TPU v7x, 128 devices: a whole 4x4x4 slice. The times are simulated.
128 devices in a mesh: row: 16 (over y, x), col: 8 (over z, core).
Axes of the slice: x: 4, y: 4, z: 4, core: 2. Of those that a mesh axis runs over, the one named last changes fastest.
Arguments:
- new_rows: float32 [32768, 2048], P('row', 'col'), may hold values from -6 to 6
- old_rows: float32 [32768, 2048], P('row', 'col'), may hold values from -6 to 6
- row_ids: int32 [32768], P('row'), may hold values from 0 to 3999999
- owner: int32 [32768, 1], P('row'), may hold values from 0 to 127; in each aligned block of 256 rows (0 to 255, 256 to 511, ...) at most 4 rows name the same one
Outputs:
- published: bfloat16 [65536, 2048], P(('row', 'col'))
- row_scale: bfloat16 [65536], P(('row', 'col'))
- published_ids: int32 [65536], P(('row', 'col'))
Inputs may be any that keep to these rules, and one draw needn't show every extreme that they name: Within one aligned block of 256 rows no owner is named more than 4 times, and in some block some owner is named exactly 4 times.
All inputs are finite; a program needn't handle non-finite values. Where the computation divides by a largest or mean magnitude, that divisor is 1e-20 or more.
Results may differ from a plain program's by a relative error of at most 0.005.
Values may be sent and summed in bfloat16 or wider, within the bound.
A program may use at most 64 MiB of HBM per device.

v0:
```python
import math

import jax
import jax.numpy as jnp
from jax import lax
from jax.sharding import PartitionSpec as P

EPSILON = 1e-06


def parity_table(size):
    index_line = lax.iota(jnp.int32, size)
    common_bits = index_line[:, None] & index_line[None, :]
    parity = jnp.zeros_like(common_bits)
    for bit_number in range(max(size.bit_length() - 1, 0)):
        parity = parity ^ common_bits >> bit_number & 1
    return 1 - 2 * parity


def deliver(parcels):
    return (
        lax.all_to_all(parcels[0], ("row", "col"), split_axis=0, concat_axis=0, tiled=True),
        lax.all_to_all(parcels[1], ("row", "col"), split_axis=0, concat_axis=0, tiled=True),
        lax.all_to_all(parcels[2], ("row", "col"), split_axis=0, concat_axis=0, tiled=True),
    )


def quantize(full_rows, width):
    rotated = jnp.dot(
        full_rows, parity_table(width).astype(jnp.bfloat16), preferred_element_type=jnp.float32
    ) * (1.0 / math.sqrt(width))
    peak_value = jnp.max(jnp.abs(rotated), axis=1)
    codes = (rotated / (peak_value[:, None] + EPSILON)).astype(jnp.bfloat16)
    return (codes, peak_value.astype(jnp.bfloat16))


def shards(new_rows, old_rows, row_ids, owner):
    columns = lax.axis_size("col")
    row_groups = lax.axis_size("row")
    devices = row_groups * columns
    rows_here = new_rows.shape[0]
    slice_width = new_rows.shape[1]
    width = slice_width * columns
    block_rows = rows_here // columns
    capacity = 2 * block_rows // devices
    slots_all = devices * capacity
    col_index = lax.axis_index("col")
    device_line = lax.iota(jnp.int32, devices)
    delta = (new_rows - old_rows).astype(jnp.bfloat16)
    position = col_index * block_rows
    full_rows = lax.all_to_all(delta, "col", split_axis=0, concat_axis=1, tiled=True)
    codes, peak_low = quantize(full_rows, width)
    block_owner = lax.dynamic_slice_in_dim(owner[:, 0], position, block_rows, 0)
    block_ids = lax.dynamic_slice_in_dim(row_ids, position, block_rows, 0)
    marks = (block_owner[:, None] == device_line[None, :]).astype(jnp.int32)
    slot = jnp.sum(marks * jnp.cumsum(marks, axis=0), axis=1) - 1
    target = block_owner * capacity + slot
    send_codes = jnp.zeros((slots_all, width), jnp.bfloat16).at[target].set(codes)
    send_scale = jnp.zeros((slots_all,), jnp.bfloat16).at[target].set(peak_low)
    send_ids = jnp.full((slots_all,), -1, jnp.int32).at[target].set(block_ids)
    got_codes, got_scale, got_ids = deliver(
        (
            send_codes.reshape(devices, capacity, width),
            send_scale.reshape(devices, capacity),
            send_ids.reshape(devices, capacity),
        )
    )
    return (
        got_codes.reshape(slots_all, width),
        got_scale.reshape(slots_all),
        got_ids.reshape(slots_all),
    )


def solution(mesh):
    return jax.shard_map(
        shards,
        mesh=mesh,
        in_specs=(P("row", "col"), P("row", "col"), P("row"), P("row", None)),
        out_specs=(P(("row", "col"), None), P(("row", "col")), P(("row", "col"))),
        check_vma=False,
    )
```

profile of v0, /device:TPU:1, one launch (start us, length us, event | category | flops | bytes accessed | tf_op | source)
XLA Modules:
  0.0 117.9 jit_solution(4121013478186261745)
XLA Ops:
  0.6 3.5 %subtract_convert_fusion.4 = bf16[2048,256]{1,0:T(8,128)(2,1)} fusion(f32[2048,256]{1,0:T(8,128)} %param.4, f32[2048,256]{1,0:T(8,128)} %param.5), kind=kLoop, calls=%fused_computation.8 | loop fusion | flops 1048576 | bytes 5242880 | tf_op jit(solution)/shard_map/convert_element_type | solution.py:49
  4.1 6.8 %all-to-all-start = ((bf16[8,256,256]{2,1,0:T(8,128)(2,1)}), bf16[8,256,256]{2,1,0:T(8,128)(2,1)S(1)}, u32[]{:S(2)}, u32[]{:S(2)}) async-start(bf16[8,256,256]{2,1,0:T(8,128)(2,1)} %bitcast.7), calls=%async_computation | async-start | bytes 2097152 | tf_op jit(solution)/shard_map/all_to_all | solution.py:51
  10.9 0.7 constant_dynamic-slice_fusion
  11.6 0.1 copy.12
  11.7 0.2 fusion.5
  12.0 0.8 dynamic_slice.7
  12.8 0.2 fusion.6
  13.0 0.7 compare_select_fusion
  13.7 1.4 %scatter_custom_fusion.2 = s32[512]{0:T(512)S(1)} fusion(s32[256]{0:T(256)S(1)} %bitcast.28, s32[256]{0:T(256)S(1)} %dynamic_slice.7, s32[]{:T(128)} %constant.26.clone.1), kind=kCustom, calls=%fused_computation.22 | custom fusion | bytes 2052 | tf_op jit(solution)/shard_map/scatter | solution.py:60
  15.1 0.7 all_to_all.36
  15.8 10.2 %all-to-all-done = bf16[8,256,256]{2,1,0:T(8,128)(2,1)S(1)} async-done(((bf16[8,256,256]{2,1,0:T(8,128)(2,1)}), bf16[8,256,256]{2,1,0:T(8,128)(2,1)S(1)}, u32[]{:S(2)}, u32[]{:S(2)}) %all-to-all-start) | async-done | bytes 1048608 | tf_op jit(solution)/shard_map/all_to_all | solution.py:51
  26.0 8.0 %all-to-all-start.3 = ((s32[128,1,4]{2,1,0:T(1,128)}), s32[128,1,4]{2,1,0:T(1,128)S(1)}, u32[]{:S(2)}, u32[]{:S(2)}) async-start(s32[128,1,4]{2,1,0:T(1,128)} %bitcast.10), calls=%async_computation.3 | async-start | bytes 131072 | tf_op jit(solution)/shard_map/all_to_all | solution.py:24
  34.0 0.5 copy.14
  34.6 22.5 %abs_reduce_fusion = (f32[256]{0:T(256)S(1)}, f32[256,2048]{1,0:T(8,128)}) fusion(bf16[256,2048]{0,1:T(8,128)(2,1)S(1)} %bitcast.21), kind=kOutput, calls=%fused_computation.7 | convolution fusion | flops 2300051200 | bytes 3146752 | tf_op jit(solution)/shard_map/dot_general | solution.py:29
  57.1 2.2 %scatter_custom_fusion.1 = bf16[512]{0:T(512)(128)(2,1)S(1)} fusion(s32[256]{0:T(256)S(1)} %bitcast.29, bf16[256]{0:T(256)(128)(2,1)S(1)} %get-tuple-element.3, bf16[]{:T(256)} %constant.20.clone.1), kind=kCustom, calls=%fused_computation.24 | custom fusion | bytes 1026 | tf_op jit(solution)/shard_map/scatter | solution.py:59
  59.3 0.8 all_to_all.38
  60.0 0.0 all-to-all-done.3
  60.0 9.8 %all-to-all-start.2 = ((bf16[128,1,4]{2,1,0:T(2,128)(2,1)}), bf16[128,1,4]{2,1,0:T(2,128)(2,1)S(1)}, u32[]{:S(2)}, u32[]{:S(2)}) async-start(bf16[128,1,4]{2,1,0:T(2,128)(2,1)} %all_to_all.38), calls=%async_computation.2 | async-start | bytes 131072 | tf_op jit(solution)/shard_map/all_to_all | solution.py:23
  69.8 3.9 %scatter_custom_fusion = bf16[512,2048]{1,0:T(8,128)(2,1)S(1)} fusion(s32[256]{0:T(256)S(1)} %bitcast.30, f32[256,2048]{1,0:T(8,128)} %get-tuple-element.6, f32[256]{0:T(256)S(1)} %get-tuple-element.4, bf16[]{:T(256)} %constant.20.clone.1), kind=kCustom, calls=%fused_computation.9 | custom fusion | flops 1048576 | bytes 4195330 | tf_op jit(solution)/shard_map/scatter | solution.py:58
  73.7 2.2 %reshape.63 = bf16[128,4,2048]{2,1,0:T(4,128)(2,1)} reshape(bf16[512,2048]{1,0:T(8,128)(2,1)S(1)} %scatter_custom_fusion) | data formatting | bytes 4194304 | tf_op jit(solution)/shard_map/reshape | solution.py:63
  75.9 3.3 %all-to-all-done.2 = bf16[128,1,4]{2,1,0:T(2,128)(2,1)S(1)} async-done(((bf16[128,1,4]{2,1,0:T(2,128)(2,1)}), bf16[128,1,4]{2,1,0:T(2,128)(2,1)S(1)}, u32[]{:S(2)}, u32[]{:S(2)}) %all-to-all-start.2) | async-done | bytes 1056 | tf_op jit(solution)/shard_map/all_to_all | solution.py:23
  79.2 6.5 %all-to-all-start.1 = ((bf16[128,4,2048]{2,1,0:T(4,128)(2,1)}), bf16[128,4,2048]{2,1,0:T(4,128)(2,1)S(1)}, u32[]{:S(2)}, u32[]{:S(2)}) async-start(bf16[128,4,2048]{2,1,0:T(4,128)(2,1)} %reshape.63), calls=%async_computation.1 | async-start | bytes 4194304 | tf_op jit(solution)/shard_map/all_to_all | solution.py:22
  85.7 0.5 broadcast.70
  86.2 0.8 reduce.4
  87.0 0.7 reshape.66
  87.7 0.2 reduce
  87.9 0.7 reshape.65
  88.6 27.4 %all-to-all-done.1 = bf16[128,4,2048]{2,1,0:T(4,128)(2,1)S(1)} async-done(((bf16[128,4,2048]{2,1,0:T(4,128)(2,1)}), bf16[128,4,2048]{2,1,0:T(4,128)(2,1)S(1)}, u32[]{:S(2)}, u32[]{:S(2)}) %all-to-all-start.1) | async-done | bytes 2097184 | tf_op jit(solution)/shard_map/all_to_all | solution.py:22
  115.9 2.0 %reshape.64 = bf16[512,2048]{1,0:T(8,128)(2,1)} reshape(bf16[128,4,2048]{2,1,0:T(4,128)(2,1)S(1)} %all-to-all-done.1) | data formatting | bytes 4194304 | tf_op jit(solution)/shard_map/reshape | solution.py:69
  (8 shorter events, 0.1 us)
Async XLA Ops:
  4.1 21.9 %all-to-all-start = ((bf16[8,256,256]{2,1,0:T(8,128)(2,1)}), bf16[8,256,256]{2,1,0:T(8,128)(2,1)S(1)}, u32[]{:S(2)}, u32[]{:S(2)}) async-start(bf16[8,256,256]{2,1,0:T(8,128)(2,1)} %bitcast.7), calls=%async_computation | async-start | bytes 2097152 | tf_op jit(solution)/shard_map/all_to_all | solution.py:51
  26.0 34.0 %all-to-all-start.3 = ((s32[128,1,4]{2,1,0:T(1,128)}), s32[128,1,4]{2,1,0:T(1,128)S(1)}, u32[]{:S(2)}, u32[]{:S(2)}) async-start(s32[128,1,4]{2,1,0:T(1,128)} %bitcast.10), calls=%async_computation.3 | async-start | bytes 131072 | tf_op jit(solution)/shard_map/all_to_all | solution.py:24
  60.0 19.2 %all-to-all-start.2 = ((bf16[128,1,4]{2,1,0:T(2,128)(2,1)}), bf16[128,1,4]{2,1,0:T(2,128)(2,1)S(1)}, u32[]{:S(2)}, u32[]{:S(2)}) async-start(bf16[128,1,4]{2,1,0:T(2,128)(2,1)} %all_to_all.38), calls=%async_computation.2 | async-start | bytes 131072 | tf_op jit(solution)/shard_map/all_to_all | solution.py:23
  79.2 36.8 %all-to-all-start.1 = ((bf16[128,4,2048]{2,1,0:T(4,128)(2,1)}), bf16[128,4,2048]{2,1,0:T(4,128)(2,1)S(1)}, u32[]{:S(2)}, u32[]{:S(2)}) async-start(bf16[128,4,2048]{2,1,0:T(4,128)(2,1)} %reshape.63), calls=%async_computation.1 | async-start | bytes 4194304 | tf_op jit(solution)/shard_map/all_to_all | solution.py:22
where the time goes:
time: 118 us
  waiting for transfers between devices  40.9 us (35%)
  starting transfers between devices  31.1 us (26%)
  matrix products  22.5 us (19%)
  local copies, waits for them, and re-layouts  13.2 us (11%)
  other arithmetic  9.56 us (8%)
    all_to_all x1, waiting for transfers between devices, deliver(): lax.all_to_all(parcels[0], ('row', 'col'), split_axis=0, concat_axis=0, t...  27.4 us
    dot_general x1, matrix products, quantize(): jnp.dot(full_rows, parity_table(width).astype(jnp.bfloat16), preferred_el...  22.5 us
    all_to_all x1, waiting for transfers between devices, shards(): lax.all_to_all(delta, 'col', split_axis=0, concat_axis=1, tiled=True)  10.2 us
    all_to_all x1, starting transfers between devices, deliver(): lax.all_to_all(parcels[1], ('row', 'col'), split_axis=0, concat_axis=0, t...  9.76 us
    all_to_all x1, starting transfers between devices, deliver(): lax.all_to_all(parcels[2], ('row', 'col'), split_axis=0, concat_axis=0, t...  7.99 us
    all_to_all x1, starting transfers between devices, shards(): lax.all_to_all(delta, 'col', split_axis=0, concat_axis=1, tiled=True)  6.81 us
    all_to_all x1, starting transfers between devices, deliver(): lax.all_to_all(parcels[0], ('row', 'col'), split_axis=0, concat_axis=0, t...  6.5 us
    scatter x1, other arithmetic, shards(): jnp.zeros((slots_all, width), jnp.bfloat16).at[target].set(codes)  3.94 us
  transfers between devices with their start and end apart: 4, of which 3 were waited for; matrix products, arithmetic and copies ran while one was open for 33% of the time, Pallas kernels for 0%

commit v1 on v0

v1 whole, which is shorter than its diff:
```python
import functools
import math

import jax
import jax.numpy as jnp
from jax import lax
from jax.experimental import pallas as pl
from jax.experimental.pallas import tpu as pltpu
from jax.sharding import PartitionSpec as P

EPSILON = 1e-06
MESH = pl.DeviceIdType.MESH
BF16, F32, I32 = jnp.bfloat16, jnp.float32, jnp.int32

N_ROW, N_COL = 16, 8
DEVICES = N_ROW * N_COL
CAP = 4
BLK = 256
SLICE = 256
D = SLICE * N_COL
ROWS_HERE = BLK * N_COL
CHUNK = CAP * N_COL
SLOTS = CHUNK * N_ROW
PAIRS = N_COL // 2
BATCH = 4


def parity_signs(size):
    common = lax.broadcasted_iota(I32, (size, size), 0) & lax.broadcasted_iota(I32, (size, size), 1)
    for shift in (4, 2, 1):
        common = common ^ (common >> shift)
    return (1 - 2 * (common & 1)).astype(F32).astype(BF16)


def kernel(
    new_ref, old_ref, owner_ref, ids_ref,
    out_ref, scale_ref, oid_ref,
    fresh, stale, delta, send, recv, codes, peaks, table, ids_send, ids_recv,
    load_sem, send_sem, recv_sem, self_sem, ids_send_sem, ids_recv_sem, ids_self_sem, out_sem,
):
    row = lax.axis_index("row")
    col = lax.axis_index("col")
    y, x = row // 4, row % 4
    z, core = col // 2, col % 2

    def ahead(step):
        return ((y + step // 4) % 4) * 4 + (x + step % 4) % 4

    def behind(step):
        return ((y + 4 - step // 4) % 4) * 4 + (x + 4 - step % 4) % 4

    def column(step):
        return ((z + step // 2) % 4) * 2 + (core + step) % 2

    def loads(pair):
        part = pl.ds(pair * 2 * BLK, 2 * BLK)
        return (
            pltpu.make_async_copy(new_ref.at[part], fresh.at[part], load_sem.at[pair]),
            pltpu.make_async_copy(old_ref.at[part], stale.at[part], load_sem.at[pair + PAIRS]),
        )

    for pair in range(PAIRS):
        for copy in loads(pair):
            copy.start()

    barrier = pltpu.get_barrier_semaphore()

    def greet(number, _):
        pl.semaphore_signal(
            barrier, inc=1, device_id=(ahead(number // N_COL), column(number % N_COL)), device_id_type=MESH
        )
        return 0

    lax.fori_loop(1, DEVICES, greet, 0)

    owner_lines = []
    marks = []
    for block in range(N_COL):
        line = jnp.concatenate([owner_ref[2 * block:2 * block + 1, :], owner_ref[2 * block + 1:2 * block + 2, :]], axis=1)
        owner_lines.append(line)
        marks.append(jnp.where(lax.broadcasted_iota(I32, (DEVICES, BLK), 0) == line, 1.0, 0.0))
    earlier = jnp.where(
        lax.broadcasted_iota(I32, (BLK, BLK), 0) < lax.broadcasted_iota(I32, (BLK, BLK), 1), 1.0, 0.0
    ).astype(BF16)
    slots = []
    for block in range(N_COL):
        counts = jnp.dot(marks[block].astype(BF16), earlier, preferred_element_type=F32)
        slots.append(jnp.sum(marks[block] * counts, axis=0, keepdims=True).astype(I32))
    keys = []
    for pair in range(PAIRS):
        first, second = 2 * pair, 2 * pair + 1
        keys.append(jnp.concatenate(
            [owner_lines[first] * (2 * CAP) + slots[first], owner_lines[second] * (2 * CAP) + CAP + slots[second]], axis=1
        ))

    for pair in range(PAIRS):
        for copy in loads(pair):
            copy.wait()
        part = pl.ds(pair * 2 * BLK, 2 * BLK)
        delta[part, :] = (fresh[part, :] - stale[part, :]).astype(BF16)

    pl.semaphore_wait(barrier, DEVICES - 1)

    def chunk_copy(step, other):
        return pltpu.make_async_remote_copy(
            src_ref=send.at[step * N_COL + other],
            dst_ref=recv.at[col, pl.ds(row * CHUNK, CHUNK)],
            send_sem=send_sem,
            recv_sem=recv_sem.at[step],
            device_id=(ahead(step), column(other)),
            device_id_type=MESH,
        )

    self_copy = pltpu.make_async_copy(send.at[0], recv.at[col, pl.ds(row * CHUNK, CHUNK)], self_sem)
    span = N_COL * 2 * CAP
    for batch in range(N_ROW // BATCH):
        packed = []
        for pair in range(PAIRS):
            picks = []
            for inner in range(BATCH):
                base = ahead(batch * BATCH + inner) * span
                line = lax.broadcasted_iota(I32, (span, 2 * BLK), 0)
                step = line // (2 * CAP)
                there = ((z + step // 2) % 4) * 2 + (core + step) % 2
                target = base + there * (2 * CAP) + line % (2 * CAP)
                picks.append(jnp.where(target == keys[pair], 1.0, 0.0).astype(BF16))
            rows = jnp.dot(
                jnp.concatenate(picks, axis=0), delta[pair * 2 * BLK:(pair + 1) * 2 * BLK, :], preferred_element_type=F32
            )
            packed.append(rows.reshape(BATCH * N_COL, 2 * CAP, SLICE))
        for half in range(PAIRS // 2):
            send[batch * BATCH * N_COL:(batch + 1) * BATCH * N_COL, half * 16:(half + 1) * 16, :] = jnp.concatenate(
                [packed[2 * half], packed[2 * half + 1]], axis=1
            ).astype(BF16)

        def start(number, _):
            chunk_copy(number // N_COL, number % N_COL).start()
            return 0

        if batch == 0:
            self_copy.start()
            lax.fori_loop(1, BATCH * N_COL, start, 0)
        else:
            lax.fori_loop(batch * BATCH * N_COL, (batch + 1) * BATCH * N_COL, start, 0)

    all_owners = jnp.concatenate(owner_lines, axis=1)
    all_slots = jnp.concatenate(slots, axis=1)
    lane = lax.broadcasted_iota(I32, (1, ROWS_HERE), 1)
    place = (row % 4) * CHUNK + (lane // BLK) * CAP + all_slots
    at_place = jnp.where(lax.broadcasted_iota(I32, (128, ROWS_HERE), 0) == place, 1.0, 0.0).astype(BF16)
    values = jnp.concatenate([ids_ref[i:i + 1, :] for i in range(ROWS_HERE // 128)], axis=1) + 1
    group = lax.broadcasted_iota(I32, (N_ROW, ROWS_HERE), 0)
    there = ((y + group // 4) % 4) * 4 + (x + group % 4) % 4
    mine = all_owners == there * N_COL + col
    pieces = [jnp.where(mine, part.astype(F32), 0.0).astype(BF16) for part in (values >> 16, (values >> 8) & 255, values & 255)]
    sums = lax.dot_general(
        jnp.concatenate(pieces, axis=0), at_place, (((1,), (1,)), ((), ())), preferred_element_type=F32
    )
    found = (sums[:N_ROW] * 65536.0 + sums[N_ROW:2 * N_ROW] * 256.0 + sums[2 * N_ROW:]).astype(I32)
    for step in range(N_ROW):
        ids_send[step] = found[step:step + 1, :]

    def ids_copy(step):
        return pltpu.make_async_remote_copy(
            src_ref=ids_send.at[step],
            dst_ref=ids_recv.at[row],
            send_sem=ids_send_sem,
            recv_sem=ids_recv_sem,
            device_id=(ahead(step), col),
            device_id_type=MESH,
        )

    ids_self = pltpu.make_async_copy(ids_send.at[0], ids_recv.at[row], ids_self_sem)
    ids_self.start()

    def start_ids(step, _):
        ids_copy(step).start()
        return 0

    lax.fori_loop(1, N_ROW, start_ids, 0)

    table[...] = parity_signs(SLICE)

    def out_copy(source):
        part = pl.ds(source * CHUNK, CHUNK)
        return pltpu.make_async_copy(codes.at[part], out_ref.at[part], out_sem)

    def rotate(step):
        source = behind(step)
        part = pl.ds(pl.multiple_of(source * CHUNK, CHUNK), CHUNK)
        got = recv[:, part, :].reshape(N_COL * CHUNK, SLICE)
        inner = jnp.dot(got, table[...], preferred_element_type=F32)
        lines = [inner[c * CHUNK:(c + 1) * CHUNK] for c in range(N_COL)]
        for gap in (1, 2, 4):
            lines = [
                lines[c] + lines[c + gap] if not c & gap else lines[c - gap] - lines[c] for c in range(N_COL)
            ]
        top = functools.reduce(jnp.maximum, [jnp.abs(line) for line in lines])
        peak = jnp.max(top, axis=1, keepdims=True) * (1.0 / math.sqrt(D))
        peaks[part, :] = jnp.broadcast_to(peak, (CHUNK, 128))
        factor = (1.0 / math.sqrt(D)) / (peak + EPSILON)
        for c in range(N_COL):
            codes[part, c * SLICE:(c + 1) * SLICE] = (lines[c] * factor).astype(BF16)
        out_copy(source).start()

    pltpu.make_async_copy(send.at[pl.ds(0, N_COL - 1)], send.at[pl.ds(0, N_COL - 1)], recv_sem.at[0]).wait()
    self_copy.wait()
    rotate(0)

    def turn(step, _):
        part = pl.ds(0, N_COL)
        pltpu.make_async_copy(send.at[part], send.at[part], recv_sem.at[step]).wait()
        rotate(step)
        return 0

    lax.fori_loop(1, N_ROW, turn, 0)

    diagonal = lax.broadcasted_iota(I32, (128, 128), 0) == lax.broadcasted_iota(I32, (128, 128), 1)
    for q in range(SLOTS // 128):
        scale_ref[q:q + 1, :] = jnp.sum(jnp.where(diagonal, peaks[q * 128:(q + 1) * 128, :], 0.0), axis=0, keepdims=True)

    ids_self.wait()
    others = pl.ds(0, N_ROW - 1)
    pltpu.make_async_copy(ids_send.at[others], ids_send.at[others], ids_recv_sem).wait()
    for q in range(SLOTS // 128):
        oid_ref[q:q + 1, :] = ids_recv[4 * q] + ids_recv[4 * q + 1] + ids_recv[4 * q + 2] + ids_recv[4 * q + 3] - 1

    pltpu.make_async_copy(codes, out_ref, out_sem).wait()
    everyone = pl.ds(0, DEVICES - 1)
    pltpu.make_async_copy(send.at[everyone], send.at[everyone], send_sem).wait()
    pltpu.make_async_copy(ids_send.at[others], ids_send.at[others], ids_send_sem).wait()


def shards(new_rows, old_rows, row_ids, owner):
    vmem = pl.BlockSpec(memory_space=pltpu.VMEM)
    anywhere = pl.BlockSpec(memory_space=pl.ANY)
    published, scale, ids = pl.pallas_call(
        kernel,
        out_shape=(
            jax.ShapeDtypeStruct((SLOTS, D), BF16),
            jax.ShapeDtypeStruct((SLOTS // 128, 128), F32),
            jax.ShapeDtypeStruct((SLOTS // 128, 128), I32),
        ),
        in_specs=[anywhere, anywhere, vmem, vmem],
        out_specs=(anywhere, vmem, vmem),
        scratch_shapes=[
            pltpu.VMEM((ROWS_HERE, SLICE), F32),
            pltpu.VMEM((ROWS_HERE, SLICE), F32),
            pltpu.VMEM((ROWS_HERE, SLICE), BF16),
            pltpu.VMEM((DEVICES, CHUNK, SLICE), BF16),
            pltpu.VMEM((N_COL, SLOTS, SLICE), BF16),
            pltpu.VMEM((SLOTS, D), BF16),
            pltpu.VMEM((SLOTS, 128), F32),
            pltpu.VMEM((SLICE, SLICE), BF16),
            pltpu.VMEM((N_ROW, 1, 128), I32),
            pltpu.VMEM((N_ROW, 1, 128), I32),
            pltpu.SemaphoreType.DMA((2 * PAIRS,)),
            pltpu.SemaphoreType.DMA,
            pltpu.SemaphoreType.DMA((N_ROW,)),
            pltpu.SemaphoreType.DMA,
            pltpu.SemaphoreType.DMA,
            pltpu.SemaphoreType.DMA,
            pltpu.SemaphoreType.DMA,
            pltpu.SemaphoreType.DMA,
        ],
        compiler_params=pltpu.CompilerParams(
            collective_id=0, has_side_effects=True, vmem_limit_bytes=40 * 1024 * 1024
        ),
    )(new_rows, old_rows, owner.reshape(ROWS_HERE // 128, 128), row_ids.reshape(ROWS_HERE // 128, 128))
    return published, scale.reshape(SLOTS).astype(BF16), ids.reshape(SLOTS)


def solution(mesh):
    return jax.shard_map(
        shards,
        mesh=mesh,
        in_specs=(P("row", "col"), P("row", "col"), P("row"), P("row", None)),
        out_specs=(P(("row", "col"), None), P(("row", "col")), P(("row", "col"))),
        check_vma=False,
    )
```

time: 118 us -> 57.3 us (0.49)
  the two profiles are of different devices: /device:TPU:1 before, /device:TPU:29 now
where the time goes in v1:
time: 57.3 us; the launch traced here: 57 us
  Pallas kernels  49.3 us (86%)
  local copies, waits for them, and re-layouts  6.46 us (11%)
  between operations  0.65 us (1%)
    pallas_call x1, Pallas kernels, shards(): pl.pallas_call(kernel, out_shape=(jax.ShapeDtypeStruct((SLOTS, D), BF16),...  49.3 us
    unnamed x10, local copies, waits for them, and re-layouts  6.46 us

profile of v1, /device:TPU:29, one launch (start us, length us, event | category | flops | bytes accessed | tf_op | source)
XLA Modules:
  0.0 57.0 jit_solution(17589513224222904656)
XLA Ops:
  0.6 0.0 copy-start
  0.6 1.6 %copy-done = f32[2048,256]{1,0:T(8,128)S(1)} copy-done((f32[2048,256]{1,0:T(8,128)S(1)}, f32[2048,256]{1,0:T(8,128)}, u32[]{:S(2)}) %copy-start) | copy-done | bytes 2097176
  2.2 0.0 copy-start.1
  2.2 1.6 %copy-done.1 = f32[2048,256]{1,0:T(8,128)S(1)} copy-done((f32[2048,256]{1,0:T(8,128)S(1)}, f32[2048,256]{1,0:T(8,128)}, u32[]{:S(2)}) %copy-start.1) | copy-done | bytes 2097176
  3.8 0.0 copy-start.2
  3.8 0.7 %copy-done.2 = s32[2048,1]{0,1:T(1,128)S(1)} copy-done((s32[2048,1]{0,1:T(1,128)S(1)}, s32[2048,1]{0,1:T(1,128)}, u32[]{:S(2)}) %copy-start.2) | copy-done | bytes 8216
  4.5 0.0 copy-start.3
  4.5 0.7 %copy-done.3 = s32[2048]{0:T(1024)S(1)} copy-done((s32[2048]{0:T(1024)S(1)}, s32[2048]{0:T(1024)}, u32[]{:S(2)}) %copy-start.3) | copy-done | bytes 8216
  5.2 49.3 %shard_map.67 = (bf16[512,2048]{1,0:T(8,128)(2,1)S(1)}, f32[4,128]{1,0:T(4,128)S(1)}, s32[4,128]{1,0:T(4,128)S(1)}) custom-call(f32[2048,256]{1,0:T(8,128)S(1)} %copy-done, f32[2048,256]{1,0:T(8,128)S(1)} %copy-done.1, s32[16,128]{1,0:T(8,128)S(1)} %bitcast.5, s32[16,128]{1,0:T(8,128)S(1)} %bitcast.6), custom_call_target="tpu_custom_call" | custom-call | tf_op jit(solution)/shard_map/pallas_call | solution.py:237
  54.5 0.6 convert_bitcast_fusion
  55.1 1.3 %copy.9 = bf16[512,2048]{1,0:T(8,128)(2,1)} copy(bf16[512,2048]{1,0:T(8,128)(2,1)S(1)} %get-tuple-element.12) | data formatting | bytes 4194304
  56.4 0.6 %copy.10 = s32[512]{0:T(512)} copy(s32[512]{0:T(512)S(1)} %bitcast.7) | data formatting | bytes 4096
Async XLA Ops:
  0.6 1.6 %copy-start = (f32[2048,256]{1,0:T(8,128)S(1)}, f32[2048,256]{1,0:T(8,128)}, u32[]{:S(2)}) copy-start(f32[2048,256]{1,0:T(8,128)} %new_ref.1) | copy-start | bytes 6291460
  2.2 1.6 %copy-start.1 = (f32[2048,256]{1,0:T(8,128)S(1)}, f32[2048,256]{1,0:T(8,128)}, u32[]{:S(2)}) copy-start(f32[2048,256]{1,0:T(8,128)} %old_ref.1) | copy-start | bytes 6291460
  3.8 0.7 %copy-start.2 = (s32[2048,1]{0,1:T(1,128)S(1)}, s32[2048,1]{0,1:T(1,128)}, u32[]{:S(2)}) copy-start(s32[2048,1]{0,1:T(1,128)} %param.7) | copy-start | bytes 24580
  4.5 0.7 %copy-start.3 = (s32[2048]{0:T(1024)S(1)}, s32[2048]{0:T(1024)}, u32[]{:S(2)}) copy-start(s32[2048]{0:T(1024)} %param.6) | copy-start | bytes 24580

commit v2 on v1

v2 whole, which is shorter than its diff:
```python
import functools
import math

import jax
import jax.numpy as jnp
from jax import lax
from jax.experimental import pallas as pl
from jax.experimental.pallas import tpu as pltpu
from jax.sharding import PartitionSpec as P

EPSILON = 1e-06
MESH = pl.DeviceIdType.MESH
BF16, F32, I32 = jnp.bfloat16, jnp.float32, jnp.int32

N_ROW, N_COL = 16, 8
DEVICES = N_ROW * N_COL
CAP = 4
BLK = 256
SLICE = 256
D = SLICE * N_COL
ROWS_HERE = BLK * N_COL
CHUNK = CAP * N_COL
SLOTS = CHUNK * N_ROW
PAIRS = N_COL // 2


def parity_signs(size):
    common = lax.broadcasted_iota(I32, (size, size), 0) & lax.broadcasted_iota(I32, (size, size), 1)
    for shift in (4, 2, 1):
        common = common ^ (common >> shift)
    return (1 - 2 * (common & 1)).astype(F32).astype(BF16)


UNITS = (
    ((1, 1), (3, 3)),
    ((1, 3), (3, 1)),
    ((1, 2), (3, 2), (1, 0), (3, 0)),
    ((2, 1), (2, 3), (0, 1), (0, 3)),
    ((0, 2), (2, 0)),
    ((2, 2), (0, 0)),
)
SPAN = N_COL * 2 * CAP


def kernel(
    new_ref, old_ref, owner_hbm, ids_hbm,
    out_ref, scale_ref, oid_ref,
    fresh, stale, owner_ref, ids_ref, delta, send, recv, codes, peaks, table, ids_send, ids_recv,
    load_sem, small_sem, plane_sem, cube_sem,
    send_sem, recv_sem, self_sem, ids_send_sem, ids_recv_sem, ids_self_sem, out_sem,
):
    row = lax.axis_index("row")
    col = lax.axis_index("col")
    y, x = row // 4, row % 4
    z, core = col // 2, col % 2

    def ahead(group):
        return ((y + group[0]) % 4) * 4 + (x + group[1]) % 4

    def behind(group):
        return ((y + 4 - group[0]) % 4) * 4 + (x + 4 - group[1]) % 4

    def column(step):
        return ((z + step // 2) % 4) * 2 + (core + step) % 2

    def loads(pair):
        part = pl.ds(pair * 2 * BLK, 2 * BLK)
        return (
            pltpu.make_async_copy(new_ref.at[part], fresh.at[part], load_sem.at[pair]),
            pltpu.make_async_copy(old_ref.at[part], stale.at[part], load_sem.at[pair + PAIRS]),
        )

    owner_load = pltpu.make_async_copy(owner_hbm, owner_ref, small_sem.at[0])
    ids_load = pltpu.make_async_copy(ids_hbm, ids_ref, small_sem.at[1])
    owner_load.start()
    for pair in range(PAIRS):
        for copy in loads(pair):
            copy.start()
    ids_load.start()

    barrier = pltpu.get_barrier_semaphore()
    along_x = [(ahead((0, step)), col) for step in (1, 2, 3)]
    along_y = [(ahead((step, 0)), col) for step in (1, 2, 3)]
    along_col = [(row, column(step)) for step in range(1, N_COL)]
    for device in along_col + along_x + along_y:
        pl.semaphore_signal(barrier, inc=1, device_id=device, device_id_type=MESH)

    owner_load.wait()
    owner_lines = []
    marks = []
    for block in range(N_COL):
        line = jnp.concatenate([owner_ref[2 * block:2 * block + 1, :], owner_ref[2 * block + 1:2 * block + 2, :]], axis=1)
        owner_lines.append(line)
        marks.append(jnp.where(lax.broadcasted_iota(I32, (DEVICES, BLK), 0) == line, 1.0, 0.0))
    earlier = jnp.where(
        lax.broadcasted_iota(I32, (BLK, BLK), 0) < lax.broadcasted_iota(I32, (BLK, BLK), 1), 1.0, 0.0
    ).astype(BF16)
    slots = []
    for block in range(N_COL):
        counts = jnp.dot(marks[block].astype(BF16), earlier, preferred_element_type=F32)
        slots.append(jnp.sum(marks[block] * counts, axis=0, keepdims=True).astype(I32))
    keys = []
    for pair in range(PAIRS):
        halves = []
        for half in range(2):
            line = owner_lines[2 * pair + half]
            group_step = ((line // 32 + 4 - y) % 4) * 4 + (line // N_COL + 4 - x) % 4
            col_step = ((line // 2 + 4 - z) % 4) * 2 + (line + core) % 2
            halves.append((group_step * N_COL + col_step) * (2 * CAP) + half * CAP + slots[2 * pair + half])
        keys.append(jnp.concatenate(halves, axis=1))

    pl.semaphore_wait(barrier, len(along_col + along_x + along_y))
    for device in along_x:
        pl.semaphore_signal(plane_sem, inc=1, device_id=device, device_id_type=MESH)

    for pair in range(PAIRS):
        for copy in loads(pair):
            copy.wait()
        part = pl.ds(pair * 2 * BLK, 2 * BLK)
        delta[part, :] = (fresh[part, :] - stale[part, :]).astype(BF16)

    pl.semaphore_wait(plane_sem, len(along_x))
    for device in along_y:
        pl.semaphore_signal(cube_sem, inc=1, device_id=device, device_id_type=MESH)

    def chunk_copy(group, index, step):
        return pltpu.make_async_remote_copy(
            src_ref=send.at[index * N_COL + step],
            dst_ref=recv.at[col, pl.ds(row * CHUNK, CHUNK)],
            send_sem=send_sem,
            recv_sem=recv_sem.at[index],
            device_id=(ahead(group), column(step)),
            device_id_type=MESH,
        )

    order = [group for unit in UNITS for group in unit]
    own = order.index((0, 0))
    self_copy = pltpu.make_async_copy(send.at[own * N_COL], recv.at[col, pl.ds(row * CHUNK, CHUNK)], self_sem)
    lines = lax.broadcasted_iota(I32, (SPAN, 2 * BLK), 0)
    index = 0
    for unit in UNITS:
        packed = []
        for pair in range(PAIRS):
            picks = [
                jnp.where(lines == keys[pair] - (group[0] * 4 + group[1]) * SPAN, 1.0, 0.0).astype(BF16) for group in unit
            ]
            rows = jnp.dot(
                jnp.concatenate(picks, axis=0), delta[pair * 2 * BLK:(pair + 1) * 2 * BLK, :], preferred_element_type=F32
            )
            packed.append(rows.reshape(len(unit) * N_COL, 2 * CAP, SLICE))
        for half in range(PAIRS // 2):
            send[index * N_COL:(index + len(unit)) * N_COL, half * 16:(half + 1) * 16, :] = jnp.concatenate(
                [packed[2 * half], packed[2 * half + 1]], axis=1
            ).astype(BF16)

        if index == 0:
            pl.semaphore_wait(cube_sem, len(along_y))

        def start(number, _, unit=unit, index=index):
            for place, group in enumerate(unit):
                step = (3 * number + 2 * place + 2) % N_COL
                if group == (0, 0):
                    @pl.when(step != 0)
                    def _():
                        chunk_copy(group, index + place, step).start()
                else:
                    chunk_copy(group, index + place, step).start()
            return 0

        lax.fori_loop(0, N_COL, start, 0)
        if (0, 0) in unit:
            self_copy.start()
        index += len(unit)

    ids_load.wait()
    all_owners = jnp.concatenate(owner_lines, axis=1)
    all_slots = jnp.concatenate(slots, axis=1)
    lane = lax.broadcasted_iota(I32, (1, ROWS_HERE), 1)
    place = (row % 4) * CHUNK + (lane // BLK) * CAP + all_slots
    at_place = jnp.where(lax.broadcasted_iota(I32, (128, ROWS_HERE), 0) == place, 1.0, 0.0).astype(BF16)
    values = jnp.concatenate([ids_ref[i:i + 1, :] for i in range(ROWS_HERE // 128)], axis=1) + 1
    number = lax.broadcasted_iota(I32, (N_ROW, ROWS_HERE), 0)
    there = ((y + number // 4) % 4) * 4 + (x + number % 4) % 4
    mine = all_owners == there * N_COL + col
    pieces = [jnp.where(mine, part.astype(F32), 0.0).astype(BF16) for part in (values >> 16, (values >> 8) & 255, values & 255)]
    sums = lax.dot_general(
        jnp.concatenate(pieces, axis=0), at_place, (((1,), (1,)), ((), ())), preferred_element_type=F32
    )
    found = (sums[:N_ROW] * 65536.0 + sums[N_ROW:2 * N_ROW] * 256.0 + sums[2 * N_ROW:]).astype(I32)
    for step in range(N_ROW):
        ids_send[step] = found[step:step + 1, :]

    ids_self = pltpu.make_async_copy(ids_send.at[0], ids_recv.at[row], ids_self_sem)
    ids_self.start()

    def start_ids(step, _):
        pltpu.make_async_remote_copy(
            src_ref=ids_send.at[step],
            dst_ref=ids_recv.at[row],
            send_sem=ids_send_sem,
            recv_sem=ids_recv_sem,
            device_id=(ahead((step // 4, step % 4)), col),
            device_id_type=MESH,
        ).start()
        return 0

    lax.fori_loop(1, N_ROW, start_ids, 0)

    table[...] = parity_signs(SLICE)

    def rotate(source):
        part = pl.ds(pl.multiple_of(source * CHUNK, CHUNK), CHUNK)
        got = recv[:, part, :].reshape(N_COL * CHUNK, SLICE)
        inner = jnp.dot(got, table[...], preferred_element_type=F32)
        lines = [inner[c * CHUNK:(c + 1) * CHUNK] for c in range(N_COL)]
        for gap in (1, 2, 4):
            lines = [
                lines[c] + lines[c + gap] if not c & gap else lines[c - gap] - lines[c] for c in range(N_COL)
            ]
        top = functools.reduce(jnp.maximum, [jnp.abs(line) for line in lines])
        peak = jnp.max(top, axis=1, keepdims=True) * (1.0 / math.sqrt(D))
        peaks[part, :] = jnp.broadcast_to(peak, (CHUNK, 128))
        factor = (1.0 / math.sqrt(D)) / (peak + EPSILON)
        for c in range(N_COL):
            codes[part, c * SLICE:(c + 1) * SLICE] = (lines[c] * factor).astype(BF16)
        pltpu.make_async_copy(codes.at[part], out_ref.at[part], out_sem).start()

    for index, group in enumerate(order):
        chunks = pl.ds(0, N_COL - 1 if index == own else N_COL)
        pltpu.make_async_copy(send.at[chunks], send.at[chunks], recv_sem.at[index]).wait()
        if index == own:
            self_copy.wait()
        rotate(behind(group))

    diagonal = lax.broadcasted_iota(I32, (128, 128), 0) == lax.broadcasted_iota(I32, (128, 128), 1)
    for q in range(SLOTS // 128):
        scale_ref[q:q + 1, :] = jnp.sum(jnp.where(diagonal, peaks[q * 128:(q + 1) * 128, :], 0.0), axis=0, keepdims=True)

    ids_self.wait()
    others = pl.ds(0, N_ROW - 1)
    pltpu.make_async_copy(ids_send.at[others], ids_send.at[others], ids_recv_sem).wait()
    for q in range(SLOTS // 128):
        oid_ref[q:q + 1, :] = ids_recv[4 * q] + ids_recv[4 * q + 1] + ids_recv[4 * q + 2] + ids_recv[4 * q + 3] - 1

    pltpu.make_async_copy(codes, out_ref, out_sem).wait()
    everyone = pl.ds(0, DEVICES - 1)
    pltpu.make_async_copy(send.at[everyone], send.at[everyone], send_sem).wait()
    pltpu.make_async_copy(ids_send.at[others], ids_send.at[others], ids_send_sem).wait()


def shards(new_rows, old_rows, row_ids, owner):
    vmem = pl.BlockSpec(memory_space=pltpu.VMEM)
    anywhere = pl.BlockSpec(memory_space=pl.ANY)
    published, scale, ids = pl.pallas_call(
        kernel,
        out_shape=(
            jax.ShapeDtypeStruct((SLOTS, D), BF16),
            jax.ShapeDtypeStruct((SLOTS // 128, 128), F32),
            jax.ShapeDtypeStruct((SLOTS // 128, 128), I32),
        ),
        in_specs=[anywhere] * 4,
        out_specs=(anywhere, vmem, vmem),
        scratch_shapes=[
            pltpu.VMEM((ROWS_HERE, SLICE), F32),
            pltpu.VMEM((ROWS_HERE, SLICE), F32),
            pltpu.VMEM((ROWS_HERE // 128, 128), I32),
            pltpu.VMEM((ROWS_HERE // 128, 128), I32),
            pltpu.VMEM((ROWS_HERE, SLICE), BF16),
            pltpu.VMEM((DEVICES, CHUNK, SLICE), BF16),
            pltpu.VMEM((N_COL, SLOTS, SLICE), BF16),
            pltpu.VMEM((SLOTS, D), BF16),
            pltpu.VMEM((SLOTS, 128), F32),
            pltpu.VMEM((SLICE, SLICE), BF16),
            pltpu.VMEM((N_ROW, 1, 128), I32),
            pltpu.VMEM((N_ROW, 1, 128), I32),
            pltpu.SemaphoreType.DMA((2 * PAIRS,)),
            pltpu.SemaphoreType.DMA((2,)),
            pltpu.SemaphoreType.REGULAR,
            pltpu.SemaphoreType.REGULAR,
            pltpu.SemaphoreType.DMA,
            pltpu.SemaphoreType.DMA((N_ROW,)),
            pltpu.SemaphoreType.DMA,
            pltpu.SemaphoreType.DMA,
            pltpu.SemaphoreType.DMA,
            pltpu.SemaphoreType.DMA,
            pltpu.SemaphoreType.DMA,
        ],
        compiler_params=pltpu.CompilerParams(
            collective_id=0, has_side_effects=True, vmem_limit_bytes=40 * 1024 * 1024
        ),
    )(*(
        pltpu.with_memory_space_constraint(array, pltpu.HBM)
        for array in (new_rows, old_rows, owner.reshape(ROWS_HERE // 128, 128), row_ids.reshape(ROWS_HERE // 128, 128))
    ))
    return published, scale.reshape(SLOTS).astype(BF16), ids.reshape(SLOTS)


def solution(mesh):
    return jax.shard_map(
        shards,
        mesh=mesh,
        in_specs=(P("row", "col"), P("row", "col"), P("row"), P("row", None)),
        out_specs=(P(("row", "col"), None), P(("row", "col")), P(("row", "col"))),
        check_vma=False,
    )
```

time: 57.3 us -> 41.7 us (0.73)
  the two profiles are of different devices: /device:TPU:29 before, /device:TPU:1 now
where the time goes in v2:
time: 41.7 us; the launch traced here: 41.6 us
  Pallas kernels  38.5 us (92%)
  local copies, waits for them, and re-layouts  1.9 us (5%)
  between operations  0.64 us (2%)
  other arithmetic  0.56 us (1%)
    pallas_call x1, Pallas kernels, shards(): pl.pallas_call(kernel, out_shape=(jax.ShapeDtypeStruct((SLOTS, D), BF16),...  38.5 us
    unnamed x2, local copies, waits for them, and re-layouts  1.9 us

profile of v2, /device:TPU:1, one launch (start us, length us, event | category | flops | bytes accessed | tf_op | source)
XLA Modules:
  0.0 41.6 jit_solution(13227930641245888956)
XLA Ops:
  0.6 38.5 %shard_map.67 = (bf16[512,2048]{1,0:T(8,128)(2,1)S(1)}, f32[4,128]{1,0:T(4,128)S(1)}, s32[4,128]{1,0:T(4,128)S(1)}) custom-call(f32[2048,256]{1,0:T(8,128)} %new_ref.1, f32[2048,256]{1,0:T(8,128)} %old_ref.1, s32[16,128]{1,0:T(8,128)} %bitcast.6, s32[16,128]{1,0:T(8,128)} %bitcast.7), custom_call_target="tpu_custom_call" | custom-call | tf_op jit(solution)/shard_map/pallas_call | solution.py:254
  39.1 0.6 %convert_bitcast_fusion = bf16[512]{0:T(512)(128)(2,1)} fusion(f32[4,128]{1,0:T(4,128)S(1)} %get-tuple-element.7), kind=kLoop, calls=%fused_computation | loop fusion | flops 512 | bytes 3072 | tf_op jit(solution)/shard_map/convert_element_type | solution.py:295
  39.7 1.3 %copy.9 = bf16[512,2048]{1,0:T(8,128)(2,1)} copy(bf16[512,2048]{1,0:T(8,128)(2,1)S(1)} %get-tuple-element.12) | data formatting | bytes 4194304
  41.0 0.6 %copy.10 = s32[512]{0:T(512)} copy(s32[512]{0:T(512)S(1)} %bitcast.5) | data formatting | bytes 4096

commit v3 on v2

v3 whole, which is shorter than its diff:
```python
import functools
import math
import random

import jax
import jax.numpy as jnp
from jax import lax
from jax.experimental import pallas as pl
from jax.experimental.pallas import tpu as pltpu
from jax.sharding import PartitionSpec as P

EPSILON = 1e-06
MESH = pl.DeviceIdType.MESH
BF16, F32, I32 = jnp.bfloat16, jnp.float32, jnp.int32

N_ROW, N_COL = 16, 8
DEVICES = N_ROW * N_COL
CAP = 4
BLK = 256
SLICE = 256
D = SLICE * N_COL
ROWS_HERE = BLK * N_COL
CHUNK = CAP * N_COL
SLOTS = CHUNK * N_ROW
PAIRS = N_COL // 2


def parity_signs(size):
    common = lax.broadcasted_iota(I32, (size, size), 0) & lax.broadcasted_iota(I32, (size, size), 1)
    for shift in (4, 2, 1):
        common = common ^ (common >> shift)
    return (1 - 2 * (common & 1)).astype(F32).astype(BF16)


def hops(chunk):
    used = []
    for step in (chunk[0] % 4, chunk[0] // 4, chunk[1] // 2):
        used += [(0, 0), (1, 0), (1, 1), (0, 1)][step]
    return used


def balanced(chunks, seed):
    rest, done, order = list(chunks), [0] * 6, []
    random.Random(seed).shuffle(rest)
    total = [max(1, sum(hops(chunk)[link] for chunk in chunks)) for link in range(6)]
    while rest:
        part = (len(order) + 1) / len(chunks)
        best = min(rest, key=lambda chunk: sum(((d + h) / t - part) ** 2 for d, h, t in zip(done, hops(chunk), total)))
        rest.remove(best)
        order.append(best)
        done = [d + h for d, h in zip(done, hops(best))]
    return order


WINDOWS = ((1, 4, 11, 14), (2, 7, 8, 13), (3, 6, 9, 12), (5, 15, 0, 10))
ARRIVAL = [group for window in WINDOWS for group in window]
BATCH = 4
SPAN = N_COL * 2 * CAP


def kernel(
    new_ref, old_ref, owner_hbm, ids_hbm,
    codes, scale_ref, oid_ref,
    fresh, stale, owner_ref, ids_ref, delta, send, recv, peaks, table, ids_send, ids_recv,
    load_sem, small_sem, x_sem, y_sem,
    send_sem, recv_sem, self_sem, ids_send_sem, ids_recv_sem, ids_self_sem,
):
    row = lax.axis_index("row")
    col = lax.axis_index("col")
    y, x = row // 4, row % 4
    z, core = col // 2, col % 2

    def flip(place, step):
        return (place, place + 1 - 2 * (place % 2), (place + 2) % 4, 3 - place)[step]

    def partner(group, step):
        return (flip(y, group // 4) * 4 + flip(x, group % 4), flip(z, step // 2) * 2 + (core + step) % 2)

    def loads(pair):
        part = pl.ds(pair * 2 * BLK, 2 * BLK)
        return (
            pltpu.make_async_copy(new_ref.at[part], fresh.at[part], load_sem.at[pair]),
            pltpu.make_async_copy(old_ref.at[part], stale.at[part], load_sem.at[pair + PAIRS]),
        )

    owner_load = pltpu.make_async_copy(owner_hbm, owner_ref, small_sem.at[0])
    ids_load = pltpu.make_async_copy(ids_hbm, ids_ref, small_sem.at[1])
    owner_load.start()
    for pair in range(PAIRS):
        for copy in loads(pair):
            copy.start()
    ids_load.start()

    barrier = pltpu.get_barrier_semaphore()
    along_x, along_y = (1, 2, 3), (4, 8, 12)

    def tell(sem, groups):
        for group in groups:
            pl.semaphore_signal(sem, inc=1, device_id=partner(group, 0), device_id_type=MESH)

    tell(barrier, along_x + along_y)
    for step in range(1, N_COL):
        pl.semaphore_signal(barrier, inc=1, device_id=partner(0, step), device_id_type=MESH)

    pl.semaphore_wait(barrier, len(along_x + along_y) + N_COL - 1)
    tell(x_sem, along_x)

    owner_load.wait()
    owner_lines = []
    marks = []
    for block in range(N_COL):
        line = jnp.concatenate([owner_ref[2 * block:2 * block + 1, :], owner_ref[2 * block + 1:2 * block + 2, :]], axis=1)
        owner_lines.append(line)
        marks.append(jnp.where(lax.broadcasted_iota(I32, (DEVICES, BLK), 0) == line, 1.0, 0.0))
    earlier = jnp.where(
        lax.broadcasted_iota(I32, (BLK, BLK), 0) < lax.broadcasted_iota(I32, (BLK, BLK), 1), 1.0, 0.0
    ).astype(BF16)
    slots = []
    for block in range(N_COL):
        counts = jnp.dot(marks[block].astype(BF16), earlier, preferred_element_type=F32)
        slots.append(jnp.sum(marks[block] * counts, axis=0, keepdims=True).astype(I32))
    keys = []
    for pair in range(PAIRS):
        halves = []
        for half in range(2):
            line = owner_lines[2 * pair + half]
            group_step = (line // N_COL) ^ row
            col_step = (line % N_COL) ^ col
            position = (((group_step % 4) ^ (group_step // 4)) * 4 + group_step // 4)
            halves.append((position * N_COL + col_step) * (2 * CAP) + half * CAP + slots[2 * pair + half])
        keys.append(jnp.concatenate(halves, axis=1))

    pl.semaphore_wait(x_sem, len(along_x))
    tell(y_sem, along_y)

    for pair in range(PAIRS):
        for copy in loads(pair):
            copy.wait()
        part = pl.ds(pair * 2 * BLK, 2 * BLK)
        delta[part, :] = (fresh[part, :] - stale[part, :]).astype(BF16)

    iota = lax.broadcasted_iota(I32, (BATCH * SPAN, 2 * BLK), 0)

    def pack(window):
        packed = []
        for pair in range(PAIRS):
            picks = jnp.where(iota == keys[pair] - window * BATCH * SPAN, 1.0, 0.0).astype(BF16)
            rows = jnp.dot(picks, delta[pair * 2 * BLK:(pair + 1) * 2 * BLK, :], preferred_element_type=F32)
            packed.append(rows.reshape(BATCH * N_COL, 2 * CAP, SLICE))
        for half in range(PAIRS // 2):
            send[window * BATCH * N_COL:(window + 1) * BATCH * N_COL, half * 16:(half + 1) * 16, :] = jnp.concatenate(
                [packed[2 * half], packed[2 * half + 1]], axis=1
            ).astype(BF16)

    def start(chunks):
        for group, step in chunks:
            position = 4 * ((group % 4) ^ (group // 4)) + group // 4
            pltpu.make_async_remote_copy(
                src_ref=send.at[position * N_COL + step],
                dst_ref=recv.at[col, pl.ds(row * CHUNK, CHUNK)],
                send_sem=send_sem,
                recv_sem=recv_sem.at[group],
                device_id=partner(group, step),
                device_id_type=MESH,
            ).start()

    pack(1)
    pack(2)
    pl.semaphore_wait(y_sem, len(along_y))
    for number, window in enumerate(WINDOWS):
        if number > 1:
            pack((number + 1) % 4)
        start(balanced([(group, step) for group in window for step in range(N_COL) if group or step], 11 + number))
    self_copy = pltpu.make_async_copy(send.at[0], recv.at[col, pl.ds(row * CHUNK, CHUNK)], self_sem)
    self_copy.start()

    ids_load.wait()
    all_owners = jnp.concatenate(owner_lines, axis=1)
    all_slots = jnp.concatenate(slots, axis=1)
    lane = lax.broadcasted_iota(I32, (1, ROWS_HERE), 1)
    place = (row % 4) * CHUNK + (lane // BLK) * CAP + all_slots
    at_place = jnp.where(lax.broadcasted_iota(I32, (128, ROWS_HERE), 0) == place, 1.0, 0.0).astype(BF16)
    values = jnp.concatenate([ids_ref[i:i + 1, :] for i in range(ROWS_HERE // 128)], axis=1) + 1
    number = lax.broadcasted_iota(I32, (N_ROW, ROWS_HERE), 0)
    there = number ^ row
    mine = all_owners == there * N_COL + col
    pieces = [jnp.where(mine, part.astype(F32), 0.0).astype(BF16) for part in (values >> 16, (values >> 8) & 255, values & 255)]
    sums = lax.dot_general(
        jnp.concatenate(pieces, axis=0), at_place, (((1,), (1,)), ((), ())), preferred_element_type=F32
    )
    found = (sums[:N_ROW] * 65536.0 + sums[N_ROW:2 * N_ROW] * 256.0 + sums[2 * N_ROW:]).astype(I32)
    for step in range(N_ROW):
        ids_send[step] = found[step:step + 1, :]

    ids_self = pltpu.make_async_copy(ids_send.at[0], ids_recv.at[row], ids_self_sem)
    ids_self.start()

    for group in range(1, N_ROW):
        pltpu.make_async_remote_copy(
            src_ref=ids_send.at[group],
            dst_ref=ids_recv.at[row],
            send_sem=ids_send_sem,
            recv_sem=ids_recv_sem,
            device_id=partner(group, 0),
            device_id_type=MESH,
        ).start()

    table[...] = parity_signs(SLICE)

    def rotate(sources):
        parts = [pl.ds(pl.multiple_of(source * CHUNK, CHUNK), CHUNK) for source in sources]
        got = jnp.concatenate([recv[:, part, :] for part in parts], axis=1)
        height = CHUNK * len(sources)
        inner = jnp.dot(got.reshape(N_COL * height, SLICE), table[...], preferred_element_type=F32)
        for place, part in enumerate(parts):
            lines = [inner[c * height + place * CHUNK:c * height + (place + 1) * CHUNK] for c in range(N_COL)]
            for gap in (1, 2, 4):
                lines = [
                    lines[c] + lines[c + gap] if not c & gap else lines[c - gap] - lines[c] for c in range(N_COL)
                ]
            top = functools.reduce(jnp.maximum, [jnp.abs(line) for line in lines])
            peak = jnp.max(top, axis=1, keepdims=True) * (1.0 / math.sqrt(D))
            peaks[part, :] = jnp.broadcast_to(peak, (CHUNK, 128))
            factor = (1.0 / math.sqrt(D)) / (peak + EPSILON)
            for c in range(N_COL):
                codes[part, c * SLICE:(c + 1) * SLICE] = (lines[c] * factor).astype(BF16)

    for first in range(0, N_ROW, 2):
        groups = ARRIVAL[first:first + 2]
        for group in groups:
            chunks = pl.ds(0, N_COL if group else N_COL - 1)
            pltpu.make_async_copy(send.at[chunks], send.at[chunks], recv_sem.at[group]).wait()
            if group == 0:
                self_copy.wait()
        rotate([partner(group, 0)[0] for group in groups])

    diagonal = lax.broadcasted_iota(I32, (128, 128), 0) == lax.broadcasted_iota(I32, (128, 128), 1)
    scale_ref[...] = jnp.concatenate([
        jnp.sum(jnp.where(diagonal, peaks[q * 128:(q + 1) * 128, :], 0.0), axis=0, keepdims=True) for q in range(SLOTS // 128)
    ], axis=0).astype(BF16)

    ids_self.wait()
    others = pl.ds(0, N_ROW - 1)
    pltpu.make_async_copy(ids_send.at[others], ids_send.at[others], ids_recv_sem).wait()
    for q in range(SLOTS // 128):
        oid_ref[q:q + 1, :] = ids_recv[4 * q] + ids_recv[4 * q + 1] + ids_recv[4 * q + 2] + ids_recv[4 * q + 3] - 1

    everyone = pl.ds(0, DEVICES - 1)
    pltpu.make_async_copy(send.at[everyone], send.at[everyone], send_sem).wait()
    pltpu.make_async_copy(ids_send.at[others], ids_send.at[others], ids_send_sem).wait()


def hand_over(codes, scale, ids, published, row_scale, published_ids, sem):
    copies = [
        pltpu.make_async_copy(codes.at[pl.ds(part, SLOTS // 8)], published.at[pl.ds(part, SLOTS // 8)], sem.at[part * 8 // SLOTS])
        for part in range(0, SLOTS, SLOTS // 8)
    ]
    copies += [
        pltpu.make_async_copy(scale, row_scale, sem.at[8]),
        pltpu.make_async_copy(ids, published_ids, sem.at[9]),
    ]
    for copy in copies:
        copy.start()
    for copy in copies:
        copy.wait()


def shards(new_rows, old_rows, row_ids, owner):
    vmem = pl.BlockSpec(memory_space=pltpu.VMEM)
    anywhere = pl.BlockSpec(memory_space=pl.ANY)
    codes, scale, ids = pl.pallas_call(
        kernel,
        out_shape=(
            jax.ShapeDtypeStruct((SLOTS, D), BF16),
            jax.ShapeDtypeStruct((SLOTS // 128, 128), BF16),
            jax.ShapeDtypeStruct((SLOTS // 128, 128), I32),
        ),
        in_specs=[anywhere] * 4,
        out_specs=(vmem, vmem, vmem),
        scratch_shapes=[
            pltpu.VMEM((ROWS_HERE, SLICE), F32),
            pltpu.VMEM((ROWS_HERE, SLICE), F32),
            pltpu.VMEM((ROWS_HERE // 128, 128), I32),
            pltpu.VMEM((ROWS_HERE // 128, 128), I32),
            pltpu.VMEM((ROWS_HERE, SLICE), BF16),
            pltpu.VMEM((DEVICES, CHUNK, SLICE), BF16),
            pltpu.VMEM((N_COL, SLOTS, SLICE), BF16),
            pltpu.VMEM((SLOTS, 128), F32),
            pltpu.VMEM((SLICE, SLICE), BF16),
            pltpu.VMEM((N_ROW, 1, 128), I32),
            pltpu.VMEM((N_ROW, 1, 128), I32),
            pltpu.SemaphoreType.DMA((2 * PAIRS,)),
            pltpu.SemaphoreType.DMA((2,)),
            pltpu.SemaphoreType.REGULAR,
            pltpu.SemaphoreType.REGULAR,
            pltpu.SemaphoreType.DMA,
            pltpu.SemaphoreType.DMA((N_ROW,)),
            pltpu.SemaphoreType.DMA,
            pltpu.SemaphoreType.DMA,
            pltpu.SemaphoreType.DMA,
            pltpu.SemaphoreType.DMA,
        ],
        compiler_params=pltpu.CompilerParams(
            collective_id=0, has_side_effects=True, vmem_limit_bytes=40 * 1024 * 1024
        ),
    )(*(
        pltpu.with_memory_space_constraint(array, pltpu.HBM)
        for array in (new_rows, old_rows, owner.reshape(ROWS_HERE // 128, 128), row_ids.reshape(ROWS_HERE // 128, 128))
    ))
    return pl.pallas_call(
        hand_over,
        out_shape=(
            jax.ShapeDtypeStruct((SLOTS, D), BF16),
            jax.ShapeDtypeStruct((SLOTS,), BF16),
            jax.ShapeDtypeStruct((SLOTS,), I32),
        ),
        in_specs=[anywhere] * 3,
        out_specs=(anywhere,) * 3,
        scratch_shapes=[pltpu.SemaphoreType.DMA((10,))],
        compiler_params=pltpu.CompilerParams(vmem_limit_bytes=1024 * 1024),
    )(*(pltpu.with_memory_space_constraint(array, pltpu.VMEM) for array in (codes, scale.reshape(SLOTS), ids.reshape(SLOTS))))


def solution(mesh):
    return jax.shard_map(
        shards,
        mesh=mesh,
        in_specs=(P("row", "col"), P("row", "col"), P("row"), P("row", None)),
        out_specs=(P(("row", "col"), None), P(("row", "col")), P(("row", "col"))),
        check_vma=False,
    )
```

time: 41.7 us -> 40.1 us (0.962)
  local copies, waits for them, and re-layouts: 1.9 us -> 0 us
  Pallas kernels: 38.5 us -> 39.4 us
  other arithmetic: 0.56 us -> 0 us
    unnamed x2 -> x0, local copies, waits for them, and re-layouts: 1.9 us -> none
    pallas_call x0 -> x1, Pallas kernels: none -> 1.4 us  [shards(): pl.pallas_call(hand_over, out_shape=(jax.ShapeDtypeStruct((SLOTS, D), BF1...]
    convert_element_type x1 -> x0, other arithmetic: 0.56 us -> none  [shards(): return (published, scale.reshape(SLOTS).astype(BF16), ids.reshape(SLOTS))]
    pallas_call x1, Pallas kernels: 38.5 us -> 38 us  [shards(): pl.pallas_call(kernel, out_shape=(jax.ShapeDtypeStruct((SLOTS, D), BF16),...]
where the time goes in v3:
time: 40.1 us; the launch traced here: 40 us
  Pallas kernels  39.4 us (98%)
  between operations  0.64 us (2%)
    pallas_call x1, Pallas kernels, shards(): pl.pallas_call(kernel, out_shape=(jax.ShapeDtypeStruct((SLOTS, D), BF16),...  38 us
    pallas_call x1, Pallas kernels, shards(): pl.pallas_call(hand_over, out_shape=(jax.ShapeDtypeStruct((SLOTS, D), BF1...  1.4 us

profile of v3, /device:TPU:1, one launch (start us, length us, event | category | flops | bytes accessed | tf_op | source)
XLA Modules:
  0.0 40.0 jit_solution(11806580141390266435)
XLA Ops:
  0.6 38.0 %shard_map.67 = (bf16[512,2048]{1,0:T(8,128)(2,1)S(1)}, bf16[4,128]{1,0:T(4,128)(2,1)S(1)}, s32[4,128]{1,0:T(4,128)S(1)}) custom-call(f32[2048,256]{1,0:T(8,128)} %new_ref.1, f32[2048,256]{1,0:T(8,128)} %old_ref.1, s32[16,128]{1,0:T(8,128)} %bitcast.6, s32[16,128]{1,0:T(8,128)} %bitcast.7), custom_call_target="tpu_custom_call" | custom-call | tf_op jit(solution)/shard_map/pallas_call | solution.py:271
  38.6 1.4 %shard_map.68 = (bf16[512,2048]{1,0:T(8,128)(2,1)}, bf16[512]{0:T(512)(128)(2,1)}, s32[512]{0:T(512)}) custom-call(bf16[512,2048]{1,0:T(8,128)(2,1)S(1)} %get-tuple-element.6.codes, bf16[512]{0:T(512)(128)(2,1)S(1)} %bitcast.5, s32[512]{0:T(512)S(1)} %bitcast.4), custom_call_target="tpu_custom_call" | custom-call | tf_op jit(solution)/shard_map/pallas_call | solution.py:310

commit v4 on v3

v4 whole, which is shorter than its diff:
```python
import functools
import math
import random

import jax
import jax.numpy as jnp
import numpy as np
from jax import lax
from jax.experimental import pallas as pl
from jax.experimental.pallas import tpu as pltpu
from jax.sharding import PartitionSpec as P

EPSILON = 1e-06
MESH = pl.DeviceIdType.MESH
BF16, F32, I32 = jnp.bfloat16, jnp.float32, jnp.int32

N_ROW, N_COL = 16, 8
DEVICES = N_ROW * N_COL
CAP = 4
BLK = 256
SLICE = 256
D = SLICE * N_COL
ROWS_HERE = BLK * N_COL
CHUNK = CAP * N_COL
SLOTS = CHUNK * N_ROW
PAIRS = N_COL // 2


def parity_signs(size):
    common = lax.broadcasted_iota(I32, (size, size), 0) & lax.broadcasted_iota(I32, (size, size), 1)
    for shift in (4, 2, 1):
        common = common ^ (common >> shift)
    return (1 - 2 * (common & 1)).astype(F32).astype(BF16)


def hops(chunk):
    used = []
    for step in (chunk[0] % 4, chunk[0] // 4, chunk[1] // 2):
        used += [(0, 0), (1, 0), (1, 1), (0, 1)][step]
    return used


def balanced(chunks, seed):
    rest, done, order = list(chunks), [0] * 6, []
    random.Random(seed).shuffle(rest)
    total = [max(1, sum(hops(chunk)[link] for chunk in chunks)) for link in range(6)]
    while rest:
        part = (len(order) + 1) / len(chunks)
        best = min(rest, key=lambda chunk: sum(((d + h) / t - part) ** 2 for d, h, t in zip(done, hops(chunk), total)))
        rest.remove(best)
        order.append(best)
        done = [d + h for d, h in zip(done, hops(best))]
    return order


ALL = [(group, step) for group in range(16) for step in range(8) if group or step]
LINES = balanced([(0, step) for step in range(1, 8)] + [(group, 0) for group in (1, 2, 3, 4, 8, 12)], 1)
PLANES = balanced(
    [(group, 0) for group in range(16) if group % 4 and group // 4] + [(group, step) for group in (1, 3, 4, 12) for step in (1, 2, 3, 6, 7)], 2
)
LAST_GROUPS = (5, 15, 7, 13)
LAST = balanced([(group, step) for group in LAST_GROUPS for step in (4, 5, 6, 7)], 3) + balanced(
    [(group, step) for group in LAST_GROUPS for step in (1, 2, 3)], 4
)
FAR = balanced([chunk for chunk in ALL if chunk not in LINES + PLANES + LAST], 5)
ORDER = LINES + PLANES + FAR + LAST
PLACE = {chunk: place for place, chunk in enumerate(ORDER + [(0, 0)])}
ARRIVAL = (0, 1, 3, 4, 12, 2, 8, 6, 9, 10, 11, 14) + LAST_GROUPS
EARLY = 12
BATCH = 32


def flip(place, step):
    return (place, place + 1 - 2 * (place % 2), (place + 2) % 4, 3 - place)[step]


def partner_row(row, group):
    return flip(row // 4, group // 4) * 4 + flip(row % 4, group % 4)


def rotate(recv, table, peaks, codes, sources, targets):
    parts = [pl.ds(pl.multiple_of(source * CHUNK, CHUNK), CHUNK) for source in sources]
    got = jnp.concatenate([recv[:, part, :] for part in parts], axis=1)
    height = CHUNK * len(sources)
    inner = jnp.dot(got.reshape(N_COL * height, SLICE), table[...], preferred_element_type=F32)
    for place, part in enumerate(parts):
        lines = [inner[c * height + place * CHUNK:c * height + (place + 1) * CHUNK] for c in range(N_COL)]
        for gap in (1, 2, 4):
            lines = [lines[c] + lines[c + gap] if not c & gap else lines[c - gap] - lines[c] for c in range(N_COL)]
        top = functools.reduce(jnp.maximum, [jnp.abs(line) for line in lines])
        peak = jnp.max(top, axis=1, keepdims=True) * (1.0 / math.sqrt(D))
        peaks[part, :] = jnp.broadcast_to(peak, (CHUNK, 128))
        factor = (1.0 / math.sqrt(D)) / (peak + EPSILON)
        for c in range(N_COL):
            codes[targets[place], c * SLICE:(c + 1) * SLICE] = (lines[c] * factor).astype(BF16)


def kernel(
    new_ref, old_ref, owner_hbm, ids_hbm, place_hbm,
    codes, recv, peaks, table, ids_recv,
    fresh, stale, owner_ref, ids_ref, place_ref, delta, send, ids_send,
    load_sem, small_sem, x_sem, y_sem, all_sem,
    send_sem, recv_sem, self_sem, ids_send_sem, ids_recv_sem, ids_self_sem,
):
    row = lax.axis_index("row")
    col = lax.axis_index("col")
    y, x = row // 4, row % 4
    z, core = col // 2, col % 2

    def partner(group, step):
        return (partner_row(row, group), flip(z, step // 2) * 2 + (core + step) % 2)

    def loads(pair):
        part = pl.ds(pair * 2 * BLK, 2 * BLK)
        return (
            pltpu.make_async_copy(new_ref.at[part], fresh.at[part], load_sem.at[pair]),
            pltpu.make_async_copy(old_ref.at[part], stale.at[part], load_sem.at[pair + PAIRS]),
        )

    owner_load = pltpu.make_async_copy(owner_hbm, owner_ref, small_sem.at[0])
    ids_load = pltpu.make_async_copy(ids_hbm, ids_ref, small_sem.at[1])
    place_load = pltpu.make_async_copy(place_hbm, place_ref, small_sem.at[2])
    owner_load.start()
    place_load.start()
    for pair in range(PAIRS):
        for copy in loads(pair):
            copy.start()
    ids_load.start()

    barrier = pltpu.get_barrier_semaphore()
    along_x, along_y = (1, 2, 3), (4, 8, 12)

    def tell(sem, groups):
        for group in groups:
            pl.semaphore_signal(sem, inc=1, device_id=partner(group, 0), device_id_type=MESH)

    tell(barrier, along_x + along_y)
    for step in range(1, N_COL):
        pl.semaphore_signal(barrier, inc=1, device_id=partner(0, step), device_id_type=MESH)

    owner_load.wait()
    me = row * N_COL + col
    owner_lines = []
    marks = []
    for block in range(N_COL):
        line = jnp.concatenate([owner_ref[2 * block:2 * block + 1, :], owner_ref[2 * block + 1:2 * block + 2, :]], axis=1) ^ me
        owner_lines.append(line)
        marks.append(jnp.where(lax.broadcasted_iota(I32, (DEVICES, BLK), 0) == line, 1.0, 0.0))
    earlier = jnp.where(
        lax.broadcasted_iota(I32, (BLK, BLK), 0) < lax.broadcasted_iota(I32, (BLK, BLK), 1), 1.0, 0.0
    ).astype(BF16)
    place_load.wait()
    places = jnp.concatenate([place_ref[...]] * (BLK // 128), axis=1)
    slots = []
    keys = []
    for block in range(N_COL):
        counts = jnp.dot(marks[block].astype(BF16), earlier, preferred_element_type=F32)
        slots.append(jnp.sum(marks[block] * counts, axis=0, keepdims=True).astype(I32))
        spot = jnp.sum(marks[block] * (counts + places), axis=0, keepdims=True).astype(I32)
        keys.append(spot + block % 2 * CAP)
    keys = [jnp.concatenate(keys[2 * pair:2 * pair + 2], axis=1) for pair in range(PAIRS)]

    pl.semaphore_wait(barrier, len(LINES))
    tell(x_sem, along_x)
    tell(y_sem, along_y)
    for pair in range(PAIRS):
        for copy in loads(pair):
            copy.wait()
        part = pl.ds(pair * 2 * BLK, 2 * BLK)
        delta[part, :] = (fresh[part, :] - stale[part, :]).astype(BF16)

    iota = lax.broadcasted_iota(I32, (BATCH * 2 * CAP, 2 * BLK), 0)

    def pack(batch):
        packed = []
        for pair in range(PAIRS):
            picks = jnp.where(iota == keys[pair] - batch * BATCH * 2 * CAP, 1.0, 0.0).astype(BF16)
            rows = jnp.dot(picks, delta[pair * 2 * BLK:(pair + 1) * 2 * BLK, :], preferred_element_type=F32)
            packed.append(rows.reshape(BATCH, 2 * CAP, SLICE))
        for half in range(PAIRS // 2):
            send[batch * BATCH:(batch + 1) * BATCH, half * 16:(half + 1) * 16, :] = jnp.concatenate(
                [packed[2 * half], packed[2 * half + 1]], axis=1
            ).astype(BF16)

    def start(first, end):
        for place in range(first, end):
            group, step = ORDER[place]
            pltpu.make_async_remote_copy(
                src_ref=send.at[place],
                dst_ref=recv.at[col, pl.ds(row * CHUNK, CHUNK)],
                send_sem=send_sem,
                recv_sem=recv_sem.at[group],
                device_id=partner(group, step),
                device_id_type=MESH,
            ).start()

    lines, planes = len(LINES), len(LINES + PLANES)
    pack(0)
    start(0, lines)
    pl.semaphore_wait(x_sem, len(along_x))
    tell(all_sem, along_y)
    pack(1)
    pl.semaphore_wait(y_sem, len(along_y))
    start(lines, planes)
    pack(2)
    pl.semaphore_wait(all_sem, len(along_y))
    start(planes, 3 * BATCH)
    pack(3)
    start(3 * BATCH, DEVICES - 1)
    self_copy = pltpu.make_async_copy(send.at[DEVICES - 1], recv.at[col, pl.ds(row * CHUNK, CHUNK)], self_sem)
    self_copy.start()

    ids_load.wait()
    all_owners = jnp.concatenate(owner_lines, axis=1)
    all_slots = jnp.concatenate(slots, axis=1)
    lane = lax.broadcasted_iota(I32, (1, ROWS_HERE), 1)
    place = (row % 4) * CHUNK + (lane // BLK) * CAP + all_slots
    at_place = jnp.where(lax.broadcasted_iota(I32, (128, ROWS_HERE), 0) == place, 1.0, 0.0).astype(BF16)
    values = jnp.concatenate([ids_ref[i:i + 1, :] for i in range(ROWS_HERE // 128)], axis=1) + 1
    number = lax.broadcasted_iota(I32, (N_ROW, ROWS_HERE), 0)
    mine = all_owners == number * N_COL
    pieces = [jnp.where(mine, part.astype(F32), 0.0).astype(BF16) for part in (values >> 16, (values >> 8) & 255, values & 255)]
    sums = lax.dot_general(
        jnp.concatenate(pieces, axis=0), at_place, (((1,), (1,)), ((), ())), preferred_element_type=F32
    )
    found = (sums[:N_ROW] * 65536.0 + sums[N_ROW:2 * N_ROW] * 256.0 + sums[2 * N_ROW:]).astype(I32)
    for step in range(N_ROW):
        ids_send[step] = found[step:step + 1, :]

    ids_self = pltpu.make_async_copy(ids_send.at[0], ids_recv.at[row], ids_self_sem)
    ids_self.start()

    for group in range(1, N_ROW):
        pltpu.make_async_remote_copy(
            src_ref=ids_send.at[group],
            dst_ref=ids_recv.at[row],
            send_sem=ids_send_sem,
            recv_sem=ids_recv_sem,
            device_id=partner(group, 0),
            device_id_type=MESH,
        ).start()

    table[...] = parity_signs(SLICE)

    def arrived(group):
        chunks = pl.ds(0, N_COL if group else N_COL - 1)
        pltpu.make_async_copy(send.at[chunks], send.at[chunks], recv_sem.at[group]).wait()
        if group == 0:
            self_copy.wait()

    for first in range(0, EARLY, 2):
        groups = ARRIVAL[first:first + 2]
        for group in groups:
            arrived(group)
        sources = [partner_row(row, group) for group in groups]
        rotate(recv, table, peaks, codes, sources, [pl.ds(pl.multiple_of(source * CHUNK, CHUNK), CHUNK) for source in sources])
    for group in ARRIVAL[EARLY:]:
        arrived(group)

    ids_self.wait()
    others = pl.ds(0, N_ROW - 1)
    pltpu.make_async_copy(ids_send.at[others], ids_send.at[others], ids_recv_sem).wait()
    everyone = pl.ds(0, DEVICES - 1)
    pltpu.make_async_copy(send.at[everyone], send.at[everyone], send_sem).wait()
    pltpu.make_async_copy(ids_send.at[others], ids_send.at[others], ids_send_sem).wait()


def finish(codes, recv, peaks, table, ids_recv, published, scale_out, ids_out, last_codes, all_peaks, scale_ref, oid_ref, sem):
    row = lax.axis_index("row")

    def slab(source):
        return pl.ds(pl.multiple_of(source * CHUNK, CHUNK), CHUNK)

    copies = []
    for place, group in enumerate(ARRIVAL[:EARLY]):
        part = slab(partner_row(row, group))
        copies.append(pltpu.make_async_copy(codes.at[part], published.at[part], sem.at[place]))
        copies[-1].start()
    for q in range(SLOTS // 128):
        oid_ref[q:q + 1, :] = ids_recv[4 * q] + ids_recv[4 * q + 1] + ids_recv[4 * q + 2] + ids_recv[4 * q + 3] - 1
    copies.append(pltpu.make_async_copy(oid_ref, ids_out, sem.at[N_ROW + 1]))
    copies[-1].start()
    all_peaks[...] = peaks[...]
    for first in range(EARLY, N_ROW, 2):
        sources = [partner_row(row, group) for group in ARRIVAL[first:first + 2]]
        targets = [pl.ds((first - EARLY + place) * CHUNK, CHUNK) for place in range(2)]
        rotate(recv, table, all_peaks, last_codes, sources, targets)
        for place in range(2):
            copies.append(
                pltpu.make_async_copy(last_codes.at[targets[place]], published.at[slab(sources[place])], sem.at[first + place])
            )
            copies[-1].start()
    diagonal = lax.broadcasted_iota(I32, (128, 128), 0) == lax.broadcasted_iota(I32, (128, 128), 1)
    scale_ref[...] = jnp.concatenate([
        jnp.sum(jnp.where(diagonal, all_peaks[q * 128:(q + 1) * 128, :], 0.0), axis=0, keepdims=True) for q in range(SLOTS // 128)
    ], axis=0).astype(BF16)
    copies.append(pltpu.make_async_copy(scale_ref, scale_out, sem.at[N_ROW]))
    copies[-1].start()
    for copy in copies:
        copy.wait()


def shards(new_rows, old_rows, row_ids, owner):
    vmem = pl.BlockSpec(memory_space=pltpu.VMEM)
    anywhere = pl.BlockSpec(memory_space=pl.ANY)
    places = np.array([PLACE[(number // N_COL, number % N_COL)] * 2 * CAP for number in range(DEVICES)], np.float32)
    places = jnp.asarray(np.repeat(places[:, None], 128, axis=1))
    received = pl.pallas_call(
        kernel,
        out_shape=(
            jax.ShapeDtypeStruct((SLOTS, D), BF16),
            jax.ShapeDtypeStruct((N_COL, SLOTS, SLICE), BF16),
            jax.ShapeDtypeStruct((SLOTS, 128), F32),
            jax.ShapeDtypeStruct((SLICE, SLICE), BF16),
            jax.ShapeDtypeStruct((N_ROW, 1, 128), I32),
        ),
        in_specs=[anywhere] * 5,
        out_specs=(vmem,) * 5,
        scratch_shapes=[
            pltpu.VMEM((ROWS_HERE, SLICE), F32),
            pltpu.VMEM((ROWS_HERE, SLICE), F32),
            pltpu.VMEM((ROWS_HERE // 128, 128), I32),
            pltpu.VMEM((ROWS_HERE // 128, 128), I32),
            pltpu.VMEM((DEVICES, 128), F32),
            pltpu.VMEM((ROWS_HERE, SLICE), BF16),
            pltpu.VMEM((DEVICES, CHUNK, SLICE), BF16),
            pltpu.VMEM((N_ROW, 1, 128), I32),
            pltpu.SemaphoreType.DMA((2 * PAIRS,)),
            pltpu.SemaphoreType.DMA((3,)),
            pltpu.SemaphoreType.REGULAR,
            pltpu.SemaphoreType.REGULAR,
            pltpu.SemaphoreType.REGULAR,
            pltpu.SemaphoreType.DMA,
            pltpu.SemaphoreType.DMA((N_ROW,)),
            pltpu.SemaphoreType.DMA,
            pltpu.SemaphoreType.DMA,
            pltpu.SemaphoreType.DMA,
            pltpu.SemaphoreType.DMA,
        ],
        compiler_params=pltpu.CompilerParams(
            collective_id=0, has_side_effects=True, vmem_limit_bytes=40 * 1024 * 1024
        ),
    )(*(
        pltpu.with_memory_space_constraint(array, pltpu.HBM)
        for array in (new_rows, old_rows, owner.reshape(ROWS_HERE // 128, 128), row_ids.reshape(ROWS_HERE // 128, 128), places)
    ))
    published, scale, ids = pl.pallas_call(
        finish,
        out_shape=(
            jax.ShapeDtypeStruct((SLOTS, D), BF16),
            jax.ShapeDtypeStruct((SLOTS // 128, 128), BF16),
            jax.ShapeDtypeStruct((SLOTS // 128, 128), I32),
        ),
        in_specs=[vmem] * 5,
        out_specs=(anywhere,) * 3,
        scratch_shapes=[
            pltpu.VMEM(((N_ROW - EARLY) * CHUNK, D), BF16),
            pltpu.VMEM((SLOTS, 128), F32),
            pltpu.VMEM((SLOTS // 128, 128), BF16),
            pltpu.VMEM((SLOTS // 128, 128), I32),
            pltpu.SemaphoreType.DMA((N_ROW + 2,)),
        ],
        compiler_params=pltpu.CompilerParams(vmem_limit_bytes=8 * 1024 * 1024),
    )(*(pltpu.with_memory_space_constraint(array, pltpu.VMEM) for array in received))
    return published, scale.reshape(SLOTS), ids.reshape(SLOTS)


def solution(mesh):
    return jax.shard_map(
        shards,
        mesh=mesh,
        in_specs=(P("row", "col"), P("row", "col"), P("row"), P("row", None)),
        out_specs=(P(("row", "col"), None), P(("row", "col")), P(("row", "col"))),
        check_vma=False,
    )
```

time: 40.1 us -> 38.7 us (0.965)
  Pallas kernels: 39.4 us -> 38 us
    pallas_call x1, Pallas kernels: 38 us -> 36.3 us  [shards(): pl.pallas_call(kernel, out_shape=(jax.ShapeDtypeStruct((SLOTS, D), BF16),...]
where the time goes in v4:
time: 38.7 us; the launch traced here: 38.6 us
  Pallas kernels  38 us (98%)
  between operations  0.64 us (2%)
    pallas_call x1, Pallas kernels, shards(): pl.pallas_call(kernel, out_shape=(jax.ShapeDtypeStruct((SLOTS, D), BF16),...  36.3 us
    pallas_call x1, Pallas kernels, shards(): pl.pallas_call(finish, out_shape=(jax.ShapeDtypeStruct((SLOTS, D), BF16),...  1.69 us

profile of v4, /device:TPU:1, one launch (start us, length us, event | category | flops | bytes accessed | tf_op | source)
XLA Modules:
  0.0 38.6 jit_solution(6287330092244876187)
XLA Ops:
  0.6 36.3 %shard_map.76 = (bf16[512,2048]{1,0:T(8,128)(2,1)S(1)}, bf16[8,512,256]{2,1,0:T(8,128)(2,1)S(1)}, f32[512,128]{1,0:T(8,128)S(1)}, bf16[256,256]{1,0:T(8,128)(2,1)S(1)}, s32[16,1,128]{2,1,0:T(1,128)S(1)}) custom-call(f32[2048,256]{1,0:T(8,128)} %new_ref.1, f32[2048,256]{1,0:T(8,128)} %old_ref.1, s32[16,128]{1,0:T(8,128)} %bitcast.4, s32[16,128]{1,0:T(8,128)} %bitcast.5, ...), custom_call_target="tpu_custom_call" | custom-call | tf_op jit(solution)/shard_map/pallas_call | solution.py:308
  36.9 1.7 %shard_map.77 = (bf16[512,2048]{1,0:T(8,128)(2,1)}, bf16[4,128]{1,0:T(4,128)(2,1)}, s32[4,128]{1,0:T(4,128)}) custom-call(bf16[512,2048]{1,0:T(8,128)(2,1)S(1)} %get-tuple-element.11.codes, bf16[8,512,256]{2,1,0:T(8,128)(2,1)S(1)} %get-tuple-element.12.recv, f32[512,128]{1,0:T(8,128)S(1)} %get-tuple-element.13.peaks, ...), custom_call_target="tpu_custom_call" | custom-call | tf_op jit(solution)/shard_map/pallas_call | solution.py:347

commit v5 on v4

--- a/solution.py
+++ b/solution.py
@@ -54,19 +54,12 @@
 
 
 ALL = [(group, step) for group in range(16) for step in range(8) if group or step]
-LINES = balanced([(0, step) for step in range(1, 8)] + [(group, 0) for group in (1, 2, 3, 4, 8, 12)], 1)
-PLANES = balanced(
-    [(group, 0) for group in range(16) if group % 4 and group // 4] + [(group, step) for group in (1, 3, 4, 12) for step in (1, 2, 3, 6, 7)], 2
-)
-LAST_GROUPS = (5, 15, 7, 13)
-LAST = balanced([(group, step) for group in LAST_GROUPS for step in (4, 5, 6, 7)], 3) + balanced(
-    [(group, step) for group in LAST_GROUPS for step in (1, 2, 3)], 4
-)
-FAR = balanced([chunk for chunk in ALL if chunk not in LINES + PLANES + LAST], 5)
-ORDER = LINES + PLANES + FAR + LAST
+FIRST = balanced([(group, step) for group in (1, 3, 4, 12) for step in (1, 2, 3, 6, 7)], 5)
+LAST = balanced([(group, 0) for group in range(1, 16)], 6)
+MIDDLE = balanced([chunk for chunk in ALL if chunk[1] and chunk not in FIRST], 5)
+ORDER = FIRST + MIDDLE + LAST
 PLACE = {chunk: place for place, chunk in enumerate(ORDER + [(0, 0)])}
-ARRIVAL = (0, 1, 3, 4, 12, 2, 8, 6, 9, 10, 11, 14) + LAST_GROUPS
-EARLY = 12
+SLAB = 64
 BATCH = 32
 
 
@@ -78,26 +71,25 @@
     return flip(row // 4, group // 4) * 4 + flip(row % 4, group % 4)
 
 
-def rotate(recv, table, peaks, codes, sources, targets):
-    parts = [pl.ds(pl.multiple_of(source * CHUNK, CHUNK), CHUNK) for source in sources]
-    got = jnp.concatenate([recv[:, part, :] for part in parts], axis=1)
-    height = CHUNK * len(sources)
-    inner = jnp.dot(got.reshape(N_COL * height, SLICE), table[...], preferred_element_type=F32)
-    for place, part in enumerate(parts):
-        lines = [inner[c * height + place * CHUNK:c * height + (place + 1) * CHUNK] for c in range(N_COL)]
+def rotate(recv, table, codes, first):
+    part = pl.ds(first, SLAB)
+    inner = jnp.dot(recv[:, part, :].reshape(N_COL * SLAB, SLICE), table[...], preferred_element_type=F32)
+    peaks = []
+    for top in range(0, SLAB, CHUNK):
+        lines = [inner[c * SLAB + top:c * SLAB + top + CHUNK] for c in range(N_COL)]
         for gap in (1, 2, 4):
             lines = [lines[c] + lines[c + gap] if not c & gap else lines[c - gap] - lines[c] for c in range(N_COL)]
-        top = functools.reduce(jnp.maximum, [jnp.abs(line) for line in lines])
-        peak = jnp.max(top, axis=1, keepdims=True) * (1.0 / math.sqrt(D))
-        peaks[part, :] = jnp.broadcast_to(peak, (CHUNK, 128))
-        factor = (1.0 / math.sqrt(D)) / (peak + EPSILON)
+        largest = functools.reduce(jnp.maximum, [jnp.abs(line) for line in lines])
+        peaks.append(jnp.max(largest, axis=1, keepdims=True) * (1.0 / math.sqrt(D)))
+        factor = (1.0 / math.sqrt(D)) / (peaks[-1] + EPSILON)
         for c in range(N_COL):
-            codes[targets[place], c * SLICE:(c + 1) * SLICE] = (lines[c] * factor).astype(BF16)
+            codes[pl.ds(first + top, CHUNK), c * SLICE:(c + 1) * SLICE] = (lines[c] * factor).astype(BF16)
+    return peaks
 
 
 def kernel(
     new_ref, old_ref, owner_hbm, ids_hbm, place_hbm,
-    codes, recv, peaks, table, ids_recv,
+    recv, table, ids_recv,
     fresh, stale, owner_ref, ids_ref, place_ref, delta, send, ids_send,
     load_sem, small_sem, x_sem, y_sem, all_sem,
     send_sem, recv_sem, self_sem, ids_send_sem, ids_recv_sem, ids_self_sem,
@@ -160,7 +152,7 @@
         keys.append(spot + block % 2 * CAP)
     keys = [jnp.concatenate(keys[2 * pair:2 * pair + 2], axis=1) for pair in range(PAIRS)]
 
-    pl.semaphore_wait(barrier, len(LINES))
+    pl.semaphore_wait(barrier, len(along_x + along_y) + N_COL - 1)
     tell(x_sem, along_x)
     tell(y_sem, along_y)
     for pair in range(PAIRS):
@@ -194,17 +186,16 @@
                 device_id_type=MESH,
             ).start()
 
-    lines, planes = len(LINES), len(LINES + PLANES)
     pack(0)
-    start(0, lines)
     pl.semaphore_wait(x_sem, len(along_x))
     tell(all_sem, along_y)
+    pl.semaphore_wait(y_sem, len(along_y))
+    start(0, len(FIRST))
     pack(1)
-    pl.semaphore_wait(y_sem, len(along_y))
-    start(lines, planes)
+    pl.semaphore_wait(all_sem, len(along_y))
+    start(len(FIRST), 2 * BATCH)
     pack(2)
-    pl.semaphore_wait(all_sem, len(along_y))
-    start(planes, 3 * BATCH)
+    start(2 * BATCH, 3 * BATCH)
     pack(3)
     start(3 * BATCH, DEVICES - 1)
     self_copy = pltpu.make_async_copy(send.at[DEVICES - 1], recv.at[col, pl.ds(row * CHUNK, CHUNK)], self_sem)
@@ -248,13 +239,7 @@
         if group == 0:
             self_copy.wait()
 
-    for first in range(0, EARLY, 2):
-        groups = ARRIVAL[first:first + 2]
-        for group in groups:
-            arrived(group)
-        sources = [partner_row(row, group) for group in groups]
-        rotate(recv, table, peaks, codes, sources, [pl.ds(pl.multiple_of(source * CHUNK, CHUNK), CHUNK) for source in sources])
-    for group in ARRIVAL[EARLY:]:
+    for group in range(N_ROW):
         arrived(group)
 
     ids_self.wait()
@@ -265,36 +250,24 @@
     pltpu.make_async_copy(ids_send.at[others], ids_send.at[others], ids_send_sem).wait()
 
 
-def finish(codes, recv, peaks, table, ids_recv, published, scale_out, ids_out, last_codes, all_peaks, scale_ref, oid_ref, sem):
-    row = lax.axis_index("row")
-
-    def slab(source):
-        return pl.ds(pl.multiple_of(source * CHUNK, CHUNK), CHUNK)
-
-    copies = []
-    for place, group in enumerate(ARRIVAL[:EARLY]):
-        part = slab(partner_row(row, group))
-        copies.append(pltpu.make_async_copy(codes.at[part], published.at[part], sem.at[place]))
-        copies[-1].start()
+def finish(recv, table, ids_recv, published, scale_out, ids_out, codes, scale_ref, oid_ref, sem):
     for q in range(SLOTS // 128):
         oid_ref[q:q + 1, :] = ids_recv[4 * q] + ids_recv[4 * q + 1] + ids_recv[4 * q + 2] + ids_recv[4 * q + 3] - 1
-    copies.append(pltpu.make_async_copy(oid_ref, ids_out, sem.at[N_ROW + 1]))
+    copies = [pltpu.make_async_copy(oid_ref, ids_out, sem.at[0])]
     copies[-1].start()
-    all_peaks[...] = peaks[...]
-    for first in range(EARLY, N_ROW, 2):
-        sources = [partner_row(row, group) for group in ARRIVAL[first:first + 2]]
-        targets = [pl.ds((first - EARLY + place) * CHUNK, CHUNK) for place in range(2)]
-        rotate(recv, table, all_peaks, last_codes, sources, targets)
-        for place in range(2):
-            copies.append(
-                pltpu.make_async_copy(last_codes.at[targets[place]], published.at[slab(sources[place])], sem.at[first + place])
-            )
-            copies[-1].start()
+    peaks = []
+    for first in range(0, SLOTS, SLAB):
+        peaks += rotate(recv, table, codes, first)
+        part = pl.ds(first, SLAB)
+        copies.append(pltpu.make_async_copy(codes.at[part], published.at[part], sem.at[2 + first // SLAB]))
+        copies[-1].start()
     diagonal = lax.broadcasted_iota(I32, (128, 128), 0) == lax.broadcasted_iota(I32, (128, 128), 1)
+    group = 128 // CHUNK
     scale_ref[...] = jnp.concatenate([
-        jnp.sum(jnp.where(diagonal, all_peaks[q * 128:(q + 1) * 128, :], 0.0), axis=0, keepdims=True) for q in range(SLOTS // 128)
+        jnp.sum(jnp.where(diagonal, jnp.concatenate(peaks[q * group:(q + 1) * group], axis=0), 0.0), axis=0, keepdims=True)
+        for q in range(SLOTS // 128)
     ], axis=0).astype(BF16)
-    copies.append(pltpu.make_async_copy(scale_ref, scale_out, sem.at[N_ROW]))
+    copies.append(pltpu.make_async_copy(scale_ref, scale_out, sem.at[1]))
     copies[-1].start()
     for copy in copies:
         copy.wait()
@@ -308,14 +281,12 @@
     received = pl.pallas_call(
         kernel,
         out_shape=(
-            jax.ShapeDtypeStruct((SLOTS, D), BF16),
             jax.ShapeDtypeStruct((N_COL, SLOTS, SLICE), BF16),
-            jax.ShapeDtypeStruct((SLOTS, 128), F32),
             jax.ShapeDtypeStruct((SLICE, SLICE), BF16),
             jax.ShapeDtypeStruct((N_ROW, 1, 128), I32),
         ),
         in_specs=[anywhere] * 5,
-        out_specs=(vmem,) * 5,
+        out_specs=(vmem,) * 3,
         scratch_shapes=[
             pltpu.VMEM((ROWS_HERE, SLICE), F32),
             pltpu.VMEM((ROWS_HERE, SLICE), F32),
@@ -351,14 +322,13 @@
             jax.ShapeDtypeStruct((SLOTS // 128, 128), BF16),
             jax.ShapeDtypeStruct((SLOTS // 128, 128), I32),
         ),
-        in_specs=[vmem] * 5,
+        in_specs=[vmem] * 3,
         out_specs=(anywhere,) * 3,
         scratch_shapes=[
-            pltpu.VMEM(((N_ROW - EARLY) * CHUNK, D), BF16),
-            pltpu.VMEM((SLOTS, 128), F32),
+            pltpu.VMEM((SLOTS, D), BF16),
             pltpu.VMEM((SLOTS // 128, 128), BF16),
             pltpu.VMEM((SLOTS // 128, 128), I32),
-            pltpu.SemaphoreType.DMA((N_ROW + 2,)),
+            pltpu.SemaphoreType.DMA((2 + SLOTS // SLAB,)),
         ],
         compiler_params=pltpu.CompilerParams(vmem_limit_bytes=8 * 1024 * 1024),
     )(*(pltpu.with_memory_space_constraint(array, pltpu.VMEM) for array in received))

time: 38.7 us -> 38 us (0.982)
  Pallas kernels: 38 us -> 37.2 us
    pallas_call x1, Pallas kernels: 36.3 us -> 35 us  [shards(): pl.pallas_call(kernel, out_shape=(jax.ShapeDtypeStruct((N_COL, SLOTS, SLI...]
    pallas_call x1, Pallas kernels: 1.69 us -> 2.19 us  [shards(): pl.pallas_call(finish, out_shape=(jax.ShapeDtypeStruct((SLOTS, D), BF16),...]
where the time goes in v5:
time: 38 us; the launch traced here: 37.8 us
  Pallas kernels  37.2 us (98%)
  between operations  0.64 us (2%)
    pallas_call x1, Pallas kernels, shards(): pl.pallas_call(kernel, out_shape=(jax.ShapeDtypeStruct((N_COL, SLOTS, SLI...  35 us
    pallas_call x1, Pallas kernels, shards(): pl.pallas_call(finish, out_shape=(jax.ShapeDtypeStruct((SLOTS, D), BF16),...  2.19 us

profile of v5, /device:TPU:1, one launch (start us, length us, event | category | flops | bytes accessed | tf_op | source)
XLA Modules:
  0.0 37.8 jit_solution(16599340391950619591)
XLA Ops:
  0.6 35.0 %shard_map.76 = (bf16[8,512,256]{2,1,0:T(8,128)(2,1)S(1)}, bf16[256,256]{1,0:T(8,128)(2,1)S(1)}, s32[16,1,128]{2,1,0:T(1,128)S(1)}) custom-call(f32[2048,256]{1,0:T(8,128)} %new_ref.1, f32[2048,256]{1,0:T(8,128)} %old_ref.1, s32[16,128]{1,0:T(8,128)} %bitcast.4, s32[16,128]{1,0:T(8,128)} %bitcast.5, f32[128,128]{1,0:T(8,128)} %constant.2.clone.place_hbm), custom_call_target="tpu_custom_call" | custom-call | tf_op jit(solution)/shard_map/pallas_call | solution.py:281
  35.6 2.2 %shard_map.77 = (bf16[512,2048]{1,0:T(8,128)(2,1)}, bf16[4,128]{1,0:T(4,128)(2,1)}, s32[4,128]{1,0:T(4,128)}) custom-call(bf16[8,512,256]{2,1,0:T(8,128)(2,1)S(1)} %get-tuple-element.9.recv, bf16[256,256]{1,0:T(8,128)(2,1)S(1)} %get-tuple-element.10.table, s32[16,1,128]{2,1,0:T(1,128)S(1)} %get-tuple-element.11.ids_recv), custom_call_target="tpu_custom_call" | custom-call | tf_op jit(solution)/shard_map/pallas_call | solution.py:318

commit v6 on v5

--- a/solution.py
+++ b/solution.py
@@ -59,7 +59,7 @@
 MIDDLE = balanced([chunk for chunk in ALL if chunk[1] and chunk not in FIRST], 5)
 ORDER = FIRST + MIDDLE + LAST
 PLACE = {chunk: place for place, chunk in enumerate(ORDER + [(0, 0)])}
-SLAB = 64
+SLAB = 32
 BATCH = 32
 
 
@@ -71,9 +71,13 @@
     return flip(row // 4, group // 4) * 4 + flip(row % 4, group % 4)
 
 
-def rotate(recv, table, codes, first):
-    part = pl.ds(first, SLAB)
-    inner = jnp.dot(recv[:, part, :].reshape(N_COL * SLAB, SLICE), table[...], preferred_element_type=F32)
+def mix(recv, table, first):
+    return jnp.dot(
+        recv[:, pl.ds(first, SLAB), :].reshape(N_COL * SLAB, SLICE), table[...], preferred_element_type=F32
+    )
+
+
+def rotate(inner, codes, first):
     peaks = []
     for top in range(0, SLAB, CHUNK):
         lines = [inner[c * SLAB + top:c * SLAB + top + CHUNK] for c in range(N_COL)]
@@ -256,8 +260,12 @@
     copies = [pltpu.make_async_copy(oid_ref, ids_out, sem.at[0])]
     copies[-1].start()
     peaks = []
+    following = mix(recv, table, 0)
     for first in range(0, SLOTS, SLAB):
-        peaks += rotate(recv, table, codes, first)
+        inner = following
+        if first + SLAB < SLOTS:
+            following = mix(recv, table, first + SLAB)
+        peaks += rotate(inner, codes, first)
         part = pl.ds(first, SLAB)
         copies.append(pltpu.make_async_copy(codes.at[part], published.at[part], sem.at[2 + first // SLAB]))
         copies[-1].start()

time: 38 us -> 37.9 us (level)
  no operation moved by 1% of the time
where the time goes in v6:
time: 37.9 us; the launch traced here: 37.8 us
  Pallas kernels  37.2 us (98%)
  between operations  0.64 us (2%)
    pallas_call x1, Pallas kernels, shards(): pl.pallas_call(kernel, out_shape=(jax.ShapeDtypeStruct((N_COL, SLOTS, SLI...  35 us
    pallas_call x1, Pallas kernels, shards(): pl.pallas_call(finish, out_shape=(jax.ShapeDtypeStruct((SLOTS, D), BF16),...  2.16 us

profile of v6, /device:TPU:1, one launch (start us, length us, event | category | flops | bytes accessed | tf_op | source)
XLA Modules:
  0.0 37.8 jit_solution(17503269932873433436)
XLA Ops:
  0.6 35.0 %shard_map.76 = (bf16[8,512,256]{2,1,0:T(8,128)(2,1)S(1)}, bf16[256,256]{1,0:T(8,128)(2,1)S(1)}, s32[16,1,128]{2,1,0:T(1,128)S(1)}) custom-call(f32[2048,256]{1,0:T(8,128)} %new_ref.1, f32[2048,256]{1,0:T(8,128)} %old_ref.1, s32[16,128]{1,0:T(8,128)} %bitcast.4, s32[16,128]{1,0:T(8,128)} %bitcast.5, f32[128,128]{1,0:T(8,128)} %constant.2.clone.place_hbm), custom_call_target="tpu_custom_call" | custom-call | tf_op jit(solution)/shard_map/pallas_call | solution.py:289
  35.6 2.2 %shard_map.77 = (bf16[512,2048]{1,0:T(8,128)(2,1)}, bf16[4,128]{1,0:T(4,128)(2,1)}, s32[4,128]{1,0:T(4,128)}) custom-call(bf16[8,512,256]{2,1,0:T(8,128)(2,1)S(1)} %get-tuple-element.9.recv, bf16[256,256]{1,0:T(8,128)(2,1)S(1)} %get-tuple-element.10.table, s32[16,1,128]{2,1,0:T(1,128)S(1)} %get-tuple-element.11.ids_recv), custom_call_target="tpu_custom_call" | custom-call | tf_op jit(solution)/shard_map/pallas_call | solution.py:326

commit v7 on v6

--- a/solution.py
+++ b/solution.py
@@ -200,11 +200,6 @@
     start(len(FIRST), 2 * BATCH)
     pack(2)
     start(2 * BATCH, 3 * BATCH)
-    pack(3)
-    start(3 * BATCH, DEVICES - 1)
-    self_copy = pltpu.make_async_copy(send.at[DEVICES - 1], recv.at[col, pl.ds(row * CHUNK, CHUNK)], self_sem)
-    self_copy.start()
-
     ids_load.wait()
     all_owners = jnp.concatenate(owner_lines, axis=1)
     all_slots = jnp.concatenate(slots, axis=1)
@@ -234,6 +229,11 @@
             device_id=partner(group, 0),
             device_id_type=MESH,
         ).start()
+
+    pack(3)
+    start(3 * BATCH, DEVICES - 1)
+    self_copy = pltpu.make_async_copy(send.at[DEVICES - 1], recv.at[col, pl.ds(row * CHUNK, CHUNK)], self_sem)
+    self_copy.start()
 
     table[...] = parity_signs(SLICE)
 

time: 37.9 us -> 37.8 us (level)
  no operation moved by 1% of the time
where the time goes in v7:
time: 37.8 us; the launch traced here: 37.7 us
  Pallas kernels  37.1 us (98%)
  between operations  0.64 us (2%)
    pallas_call x1, Pallas kernels, shards(): pl.pallas_call(kernel, out_shape=(jax.ShapeDtypeStruct((N_COL, SLOTS, SLI...  34.9 us
    pallas_call x1, Pallas kernels, shards(): pl.pallas_call(finish, out_shape=(jax.ShapeDtypeStruct((SLOTS, D), BF16),...  2.16 us

profile of v7, /device:TPU:1, one launch (start us, length us, event | category | flops | bytes accessed | tf_op | source)
XLA Modules:
  0.0 37.7 jit_solution(5729447778800633235)
XLA Ops:
  0.6 34.9 %shard_map.76 = (bf16[8,512,256]{2,1,0:T(8,128)(2,1)S(1)}, bf16[256,256]{1,0:T(8,128)(2,1)S(1)}, s32[16,1,128]{2,1,0:T(1,128)S(1)}) custom-call(f32[2048,256]{1,0:T(8,128)} %new_ref.1, f32[2048,256]{1,0:T(8,128)} %old_ref.1, s32[16,128]{1,0:T(8,128)} %bitcast.4, s32[16,128]{1,0:T(8,128)} %bitcast.5, f32[128,128]{1,0:T(8,128)} %constant.2.clone.place_hbm), custom_call_target="tpu_custom_call" | custom-call | tf_op jit(solution)/shard_map/pallas_call | solution.py:289
  35.6 2.2 %shard_map.77 = (bf16[512,2048]{1,0:T(8,128)(2,1)}, bf16[4,128]{1,0:T(4,128)(2,1)}, s32[4,128]{1,0:T(4,128)}) custom-call(bf16[8,512,256]{2,1,0:T(8,128)(2,1)S(1)} %get-tuple-element.9.recv, bf16[256,256]{1,0:T(8,128)(2,1)S(1)} %get-tuple-element.10.table, s32[16,1,128]{2,1,0:T(1,128)S(1)} %get-tuple-element.11.ids_recv), custom_call_target="tpu_custom_call" | custom-call | tf_op jit(solution)/shard_map/pallas_call | solution.py:326

commit v8 on v7

--- a/solution.py
+++ b/solution.py
@@ -255,10 +255,7 @@
 
 
 def finish(recv, table, ids_recv, published, scale_out, ids_out, codes, scale_ref, oid_ref, sem):
-    for q in range(SLOTS // 128):
-        oid_ref[q:q + 1, :] = ids_recv[4 * q] + ids_recv[4 * q + 1] + ids_recv[4 * q + 2] + ids_recv[4 * q + 3] - 1
-    copies = [pltpu.make_async_copy(oid_ref, ids_out, sem.at[0])]
-    copies[-1].start()
+    copies = []
     peaks = []
     following = mix(recv, table, 0)
     for first in range(0, SLOTS, SLAB):
@@ -269,6 +266,10 @@
         part = pl.ds(first, SLAB)
         copies.append(pltpu.make_async_copy(codes.at[part], published.at[part], sem.at[2 + first // SLAB]))
         copies[-1].start()
+    for q in range(SLOTS // 128):
+        oid_ref[q:q + 1, :] = ids_recv[4 * q] + ids_recv[4 * q + 1] + ids_recv[4 * q + 2] + ids_recv[4 * q + 3] - 1
+    copies.append(pltpu.make_async_copy(oid_ref, ids_out, sem.at[0]))
+    copies[-1].start()
     diagonal = lax.broadcasted_iota(I32, (128, 128), 0) == lax.broadcasted_iota(I32, (128, 128), 1)
     group = 128 // CHUNK
     scale_ref[...] = jnp.concatenate([

time: 37.8 us -> 37.8 us (level)
  no operation moved by 1% of the time
where the time goes in v8:
time: 37.8 us; the launch traced here: 37.7 us
  Pallas kernels  37.1 us (98%)
  between operations  0.64 us (2%)
    pallas_call x1, Pallas kernels, shards(): pl.pallas_call(kernel, out_shape=(jax.ShapeDtypeStruct((N_COL, SLOTS, SLI...  34.9 us
    pallas_call x1, Pallas kernels, shards(): pl.pallas_call(finish, out_shape=(jax.ShapeDtypeStruct((SLOTS, D), BF16),...  2.15 us

profile of v8, /device:TPU:1, one launch (start us, length us, event | category | flops | bytes accessed | tf_op | source)
XLA Modules:
  0.0 37.7 jit_solution(11158373235655504678)
XLA Ops:
  0.6 34.9 %shard_map.76 = (bf16[8,512,256]{2,1,0:T(8,128)(2,1)S(1)}, bf16[256,256]{1,0:T(8,128)(2,1)S(1)}, s32[16,1,128]{2,1,0:T(1,128)S(1)}) custom-call(f32[2048,256]{1,0:T(8,128)} %new_ref.1, f32[2048,256]{1,0:T(8,128)} %old_ref.1, s32[16,128]{1,0:T(8,128)} %bitcast.4, s32[16,128]{1,0:T(8,128)} %bitcast.5, f32[128,128]{1,0:T(8,128)} %constant.2.clone.place_hbm), custom_call_target="tpu_custom_call" | custom-call | tf_op jit(solution)/shard_map/pallas_call | solution.py:290
  35.6 2.2 %shard_map.77 = (bf16[512,2048]{1,0:T(8,128)(2,1)}, bf16[4,128]{1,0:T(4,128)(2,1)}, s32[4,128]{1,0:T(4,128)}) custom-call(bf16[8,512,256]{2,1,0:T(8,128)(2,1)S(1)} %get-tuple-element.9.recv, bf16[256,256]{1,0:T(8,128)(2,1)S(1)} %get-tuple-element.10.table, s32[16,1,128]{2,1,0:T(1,128)S(1)} %get-tuple-element.11.ids_recv), custom_call_target="tpu_custom_call" | custom-call | tf_op jit(solution)/shard_map/pallas_call | solution.py:327
